TPU v7x, 256 devices: a whole 4x4x8 slice. The times are simulated.
256 devices in a mesh: flow: 32 (over x, y, core), cross: 8 (over z).
Axes of the slice: x: 4, y: 4, z: 8, core: 2. Of those that a mesh axis runs over, the one named last changes fastest.
Arguments:
- right_side: float32 [32, 16, 2, 8, 135], P('flow', 'cross'), may hold values from -6 to 6
- start_iterate: float32 [32, 16, 2, 8, 135], P('flow', 'cross'), may hold values from -6 to 6
- inverse_blocks: float32 [32, 16, 2, 135, 135], P('flow', 'cross'), may hold values from -2 to 2
- face_blocks: float32 [32, 6, 16, 2, 135, 135], P('flow', None, 'cross'), may hold values from -2 to 2
- color_order: int32 [32, 16, 2], P('flow', 'cross'), may hold values from 0 to 1, as said below
Outputs:
- sweep: float32 [32, 16, 2, 8, 135], P('flow', 'cross')
Inputs may be any that keep to these rules, and one draw needn't show every extreme that they name: `color_order`: in every flow layer the colors form a checkerboard over cross columns and span positions: neighbours inside one layer have different colors.
All inputs are finite; a program needn't handle non-finite values.
Results may differ from a plain program's by a relative error of at most 0.0003.
Values sent between devices are 32-bit elements; how exact they have to be, the bound alone decides.
A program may use at most 128 MiB of HBM per device.

v0:
```python
import jax
import jax.numpy as jnp
from jax import lax
from jax.sharding import PartitionSpec as P


def with_halo(cells, sides, width):
    for axis, dim in sides:
        count = lax.axis_size(axis)
        ends = count - 1
        head = lax.slice_in_dim(cells, 0, width, axis=dim)
        tail = lax.slice_in_dim(cells, cells.shape[dim] - width, cells.shape[dim], axis=dim)
        cells = jnp.concatenate(
            [
                lax.ppermute(tail, axis, [(i, (i + 1) % count) for i in range(ends)]),
                cells,
                lax.ppermute(head, axis, [((i + 1) % count, i) for i in range(ends)]),
            ],
            axis=dim,
        )
    return cells


def shifted(block, axis, distance):
    devices = range(lax.axis_size(axis))
    route = [(i - distance, i) for i in devices if i - distance in devices]
    return lax.ppermute(block, axis, route)


def prefix_2(part, axis, combine, identity):
    place = lax.axis_index(axis)
    gathered = jax.tree.map(lambda a: lax.all_gather(a, axis), part)
    state = jax.tree.map(lambda a, e: jnp.zeros_like(a) + jnp.asarray(e, a.dtype), part, identity)

    def one(lap, state):
        return combine(
            state, jax.tree.map(lambda a: lax.dynamic_index_in_dim(a, lap, 0, False), gathered)
        )

    return lax.fori_loop(0, place, one, state)


def apply_blocks(blocks, vectors):
    return jnp.einsum("jkrc,jkvc->jkvr", blocks, vectors, precision=lax.Precision.HIGHEST)


def from_left(values):
    return jnp.pad(values[:-1], ((1, 0), (0, 0), (0, 0), (0, 0)))


def from_right(values):
    return jnp.pad(values[1:], ((0, 1), (0, 0), (0, 0), (0, 0)))


def from_back(values):
    return jnp.pad(values[:, :-1], ((0, 0), (1, 0), (0, 0), (0, 0)))


def from_front(values):
    return jnp.pad(values[:, 1:], ((0, 0), (0, 1), (0, 0), (0, 0)))


def sweep_layers(
    source_all,
    padded_old,
    next_old,
    inbound,
    inverse_blocks,
    face_blocks,
    color_order,
    keep_left,
    keep_right,
):

    def layer(upper, items):
        source, around, below, inverse, faces, colors = items
        old = around[1:-1]
        total = source - apply_blocks(faces[0], upper) - apply_blocks(faces[1], below)
        total = total - apply_blocks(faces[2], around[:-2]) - apply_blocks(faces[3], around[2:])
        total = (
            total - apply_blocks(faces[4], from_back(old)) - apply_blocks(faces[5], from_front(old))
        )
        first = apply_blocks(inverse, total)
        first_color = (colors == 0)[:, :, None, None]
        delta = jnp.where(first_color, first - old, jnp.zeros_like(first))
        correction = apply_blocks(faces[2], keep_left * from_left(delta)) + apply_blocks(
            faces[3], keep_right * from_right(delta)
        )
        correction = (
            correction
            + apply_blocks(faces[4], from_back(delta))
            + apply_blocks(faces[5], from_front(delta))
        )
        fresh = jnp.where(first_color, first, first - apply_blocks(inverse, correction))
        return (fresh, fresh)

    items = (source_all, padded_old, next_old, inverse_blocks, face_blocks, color_order)
    return lax.scan(layer, inbound, items)[1]


def body(right_side, start_iterate, inverse_blocks, face_blocks, color_order):
    layers, columns, spans, vectors, width = right_side.shape
    column_ids = jnp.arange(columns)
    keep_left = (column_ids != 0).astype(jnp.float32)[:, None, None, None]
    keep_right = (column_ids != columns - 1).astype(jnp.float32)[:, None, None, None]
    padded_old = with_halo(start_iterate, (("cross", 1),), 1)
    below = shifted(start_iterate, "flow", -1)
    next_old = jnp.concatenate([start_iterate[1:], below], axis=0)

    def run(inbound):
        return sweep_layers(
            right_side,
            padded_old,
            next_old,
            inbound,
            inverse_blocks,
            face_blocks,
            color_order,
            keep_left,
            keep_right,
        )

    unknowns = columns * spans * width
    basis = (
        jnp.eye(unknowns, dtype=jnp.float32)
        .reshape(unknowns, columns, spans, width)
        .transpose(1, 2, 0, 3)
    )
    empty_next = jnp.zeros((layers, columns, spans, unknowns, width), jnp.float32)
    empty_padded = jnp.zeros((layers, columns + 2, spans, unknowns, width), jnp.float32)
    response = sweep_layers(
        empty_next,
        empty_padded,
        empty_next,
        basis,
        inverse_blocks,
        face_blocks,
        color_order,
        keep_left,
        keep_right,
    )[-1]
    response = response.transpose(2, 0, 1, 3).reshape(unknowns, unknowns)
    offset = run(jnp.zeros((columns, spans, vectors, width), jnp.float32))[-1]
    offset = offset.transpose(2, 0, 1, 3).reshape(vectors, unknowns)

    def compose(earlier, later):
        mapped = jnp.dot(earlier[0], later[0], precision=lax.Precision.HIGHEST)
        moved = jnp.dot(earlier[1], later[0], precision=lax.Precision.HIGHEST) + later[1]
        return (mapped, moved)

    identity = (jnp.eye(unknowns, dtype=jnp.float32), jnp.zeros((vectors, unknowns), jnp.float32))
    prefix = prefix_2((response, offset), "flow", compose, identity)
    inbound = prefix[1].reshape(vectors, columns, spans, width).transpose(1, 2, 0, 3)
    return run(inbound)


def solution(mesh):
    return jax.shard_map(
        body,
        mesh=mesh,
        in_specs=(
            P("flow", "cross", None, None, None),
            P("flow", "cross", None, None, None),
            P("flow", "cross", None, None, None),
            P("flow", None, "cross", None, None, None),
            P("flow", "cross", None),
        ),
        out_specs=P("flow", "cross", None, None, None),
        check_vma=False,
    )
```

profile of v0, /device:TPU:126, one launch (start us, length us, event | category | flops | bytes accessed | tf_op | source)
XLA Modules:
  0.0 266.0 jit_solution(10346754219898610342)
XLA Ops:
  7.3 3.0 %fusion.97 = (f32[1,1,2,2,135,135]{5,3,4,2,1,0:T(2,128)S(1)}, f32[1,1,2,2,135,135]{5,3,4,2,1,0:T(2,128)S(1)}, f32[1,1,2,2,135,135]{5,3,4,2,1,0:T(2,128)S(1)}, f3...) fusion(f32[1,6,2,2,135,135]{5,3,4,2,1,0:T(2,128)} %param.10), kind=kLoop, calls=%fused_computation.128 | loop fusion | bytes 3499200 | tf_op jit(solution)/shard_map/while/body/eval_jaxpr/slice | solution.py:78
  27.1 2.7 %subtract_select_fusion = f32[540,2,2,135]{0,3,2,1:T(8,128)} fusion(f32[2,2,540,135]{2,3,1,0:T(8,128)S(1)} %convolution_add_fusion, f32[2,2,540,135]{2,3,1,0:T(8,128)S(1)} %get-tuple-element.170, pred[2,2]{1,0:T(4,128)(4,1)S(1)} %compare_bitcast_fusion, f32[2,2,135,135]{3,1,2,0:T(2,128)S(1)} %bitcast.109), kind=kOutput, calls=%fused_computation.6 | convolution fusion | flops 472975200 | bytes 3790804 | tf_op jit(solution)/shard_map/while/body/eval_jaxpr/jkrc,jkvc->jkvr/dot_general | solution.py:44
  29.8 2.6 all_gather_reshape.6
  32.4 2.9 %copy.39 = f32[1,540,540]{2,1,0:T(8,128)} copy(f32[1,540,540]{1,2,0:T(8,128)} %all_gather_reshape.6) | data formatting | bytes 2332800 | tf_op jit(solution)/shard_map/all_gather;reshape | solution.py:32
  40.2 5.0 %collective-permute-start.1 = (f32[1,1,2,8,135]{4,3,2,1,0:T(8,128)S(1)}, f32[1,1,2,8,135]{4,3,2,1,0:T(8,128)S(1)}, u32[]{:S(2)}, u32[]{:S(2)}) collective-permute-start(f32[1,1,2,8,135]{4,3,2,1,0:T(8,128)S(1)} %get-tuple-element.167), channel_id=1, source_target_pairs={{0,1},{1,2},{2,3},{3,4},{4,5},{5,6},{6,7},{8,9},{9,10},{10,11},{11... | collective-permute-start | bytes 25928 | tf_op jit(solution)/shard_map/ppermute | solution.py:15
  53.5 27.5 %all_gather.7 = f32[32,8,540]{2,1,0:T(8,128)} all-gather(f32[1,8,540]{2,1,0:T(8,128)} %all_gather_reshape.7), channel_id=1, replica_groups=mesh['flow'=32,'cross'=8] {'flow'}, dimensions={0}, use_global_device_ids=true | all-gather | bytes 570240 | tf_op jit(solution)/shard_map/all_gather | solution.py:32
  81.1 102.8 %all-gather.2.cloned.1.call-done = f32[32,540,540]{2,1,0:T(8,128)} async-done(((f32[1,540,540]{2,1,0:T(8,128)}), f32[32,540,540]{2,1,0:T(8,128)}) %all-gather.2.cloned.1.call-update) | async-done | bytes 37324816 | tf_op jit(solution)/shard_map/all_gather | solution.py:32
  183.8 68.5 %while.3 = (s32[]{:T(128)}, f32[8,540]{1,0:T(8,128)S(1)}, s32[]{:T(128)}, f32[32,540,540]{2,1,0:T(8,128)}, f32[32,8,540]{2,1,0:T(8,128)}, /*index=5*/s32[]{:T(128)}, s32[]{:T(128)}, s32[]{:T(128)}) while((s32[]{:T(128)}, f32[8,540]{1,0:T(8,128)S(1)}, s32[]{:T(128)}, f32[32,540,540]{2,1,0:T(8,128)}, f32[32,8,540]{2,1,0:T(8,128)}, ...), condition=%wide.region_1.2_spmd, body=%wide.region_0.1_spmd.sunk | while | flops 27997924 | bytes 1483391 | solution.py:40
  186.1 2.3 fusion.114
  188.4 2.3 fusion.114
  190.7 2.3 fusion.114
  193.0 2.3 fusion.114
  195.3 2.3 fusion.114
  197.5 2.3 fusion.114
  199.8 2.3 fusion.114
  202.1 2.3 fusion.114
  204.4 2.3 fusion.114
  206.7 2.3 fusion.114
  209.0 2.3 fusion.114
  211.2 2.3 fusion.114
  213.5 2.3 fusion.114
  215.8 2.3 fusion.114
  218.1 2.3 fusion.114
  220.4 2.3 fusion.114
  (117 shorter events, 69.0 us)
Async XLA Ops:
  6.5 12.3 %copy-start = (f32[1,2,2,135,135]{4,2,3,1,0:T(2,128)S(1)}, f32[1,2,2,135,135]{4,2,3,1,0:T(2,128)}, u32[]{:S(2)}) copy-start(f32[1,2,2,135,135]{4,2,3,1,0:T(2,128)} %param.9) | copy-start | bytes 874804
  6.5 177.3 %all-gather.2.cloned.1.call-start = ((), (), s32[]{:S(2)}) async-start(), calls=%async_computation | async-start | bytes 45957120 | tf_op jit(solution)/shard_map/all_gather | solution.py:32
  6.6 13.9 %copy-start.9 = (f32[2]{0:T(128)}, f32[2]{0:T(128)S(1)}, u32[]{:S(2)}) copy-start(f32[2]{0:T(128)S(1)} %compare_convert_fusion.1) | copy-start | bytes 28
  6.6 43.9 %copy-start.7 = (f32[2]{0:T(128)}, f32[2]{0:T(128)S(1)}, u32[]{:S(2)}) copy-start(f32[2]{0:T(128)S(1)} %compare_convert_fusion) | copy-start | bytes 28
  7.3 44.9 %copy-start.5 = (pred[2,2]{1,0:T(4,128)(4,1)}, pred[2,2]{1,0:T(4,128)(4,1)S(1)}, u32[]{:S(2)}) copy-start(pred[2,2]{1,0:T(4,128)(4,1)S(1)} %compare_bitcast_fusion) | copy-start | bytes 16
  10.4 2.5 copy-start.1
  35.3 0.8 copy-start.3
  36.1 11.4 %collective-permute-start = (f32[1,2,2,8,135]{4,3,2,1,0:T(8,128)S(1)}, f32[1,2,2,8,135]{4,3,2,1,0:T(8,128)}, u32[]{:S(2)}, u32[]{:S(2)}) collective-permute-start(f32[1,2,2,8,135]{4,3,2,1,0:T(8,128)S(1)} %copy-done.3), channel_id=1, source_target_pairs={{8,0},{16,8},{24,16},{32,24},{40,32},{48,40},{56,48},{64,56},{72,6... | collective-permute-start | bytes 51848 | tf_op jit(solution)/shard_map/ppermute | solution.py:27
  38.2 8.2 %collective-permute-start.2 = (f32[1,1,2,8,135]{4,3,2,1,0:T(8,128)S(1)}, f32[1,1,2,8,135]{4,3,2,1,0:T(8,128)S(1)}, u32[]{:S(2)}, u32[]{:S(2)}) collective-permute-start(f32[1,1,2,8,135]{4,3,2,1,0:T(8,128)S(1)} %get-tuple-element.168), channel_id=1, source_target_pairs={{1,0},{2,1},{3,2},{4,3},{5,4},{6,5},{7,6},{9,8},{10,9},{11,10},{12... | collective-permute-start | bytes 25928 | tf_op jit(solution)/shard_map/ppermute | solution.py:17
  40.2 6.7 %collective-permute-start.1 = (f32[1,1,2,8,135]{4,3,2,1,0:T(8,128)S(1)}, f32[1,1,2,8,135]{4,3,2,1,0:T(8,128)S(1)}, u32[]{:S(2)}, u32[]{:S(2)}) collective-permute-start(f32[1,1,2,8,135]{4,3,2,1,0:T(8,128)S(1)} %get-tuple-element.167), channel_id=1, source_target_pairs={{0,1},{1,2},{2,3},{3,4},{4,5},{5,6},{6,7},{8,9},{9,10},{10,11},{11... | collective-permute-start | bytes 25928 | tf_op jit(solution)/shard_map/ppermute | solution.py:15
  45.8 3.0 %copy-start.4 = (f32[1,2,2,8,135]{4,3,2,1,0:T(8,128)S(1)}, f32[1,2,2,8,135]{4,3,2,1,0:T(8,128)}, u32[]{:S(2)}) copy-start(f32[1,2,2,8,135]{4,3,2,1,0:T(8,128)} %param.7) | copy-start | bytes 51844
  46.3 1.1 copy-start.2
  46.9 3.0 %copy-start.10 = (f32[2]{0:T(128)S(1)}, f32[2]{0:T(128)}, u32[]{:S(2)}) copy-start(f32[2]{0:T(128)} %copy-done.9) | copy-start | bytes 28
  252.3 3.3 %copy-start.11 = (f32[2]{0:T(128)S(1)}, f32[2]{0:T(128)}, u32[]{:S(2)}) copy-start(f32[2]{0:T(128)} %copy-done.9) | copy-start | bytes 28
  252.3 3.9 %copy-start.8 = (f32[2]{0:T(128)S(1)}, f32[2]{0:T(128)}, u32[]{:S(2)}) copy-start(f32[2]{0:T(128)} %copy-done.7) | copy-start | bytes 28
  255.6 2.3 copy-start.6
Sparse Core Ops, SparseCore 0:
  35.5 148.3 all-gather.1
where the time goes:
time: 271 us; the launch traced here: 266 us
  waiting for transfers between devices  103 us (38%)
  matrix products  101 us (37%)
  blocking collectives  27.5 us (10%)
  between operations  13.7 us (5%)
  local copies, waits for them, and re-layouts  11 us (4%)
  starting transfers between devices  9.13 us (3%)
    all_gather x1, waiting for transfers between devices, prefix_2(): gathered = jax.tree.map(lambda a: lax.all_gather(a, axis), part)  103 us
    dot_general x30, matrix products, compose(): jnp.dot(earlier[1], later[0], precision=lax.Precision.HIGHEST) + later[1]  67.8 us
    dot_general x31, matrix products, apply_blocks(): jnp.einsum('jkrc,jkvc->jkvr', blocks, vectors, precision=lax.Precision.HI...  32.7 us
    all_gather x1, blocking collectives, prefix_2(): gathered = jax.tree.map(lambda a: lax.all_gather(a, axis), part)  27.5 us
    another operation x3, local copies, waits for them, and re-layouts, prefix_2(): gathered = jax.tree.map(lambda a: lax.all_gather(a, axis), part)  6.21 us
  transfers between devices with their start and end apart: 4, of which 1 were waited for; matrix products, arithmetic and copies ran while one was open for 3% of the time, Pallas kernels for 0%

commit v1 on v0

v1 whole, which is shorter than its diff:
```python
import functools

import jax
import jax.numpy as jnp
from jax import lax
from jax.experimental import pallas as pl
from jax.experimental.pallas import tpu as pltpu
from jax.sharding import PartitionSpec as P

MESH = pl.DeviceIdType.MESH
BF16 = jnp.bfloat16
F32 = jnp.float32
NN = (((1,), (0,)), ((), ()))
NT = (((1,), (1,)), ((), ()))

MAIN, REM, WIDE = 512, 32, 640
ROWS = MAIN + REM
TWICE = ROWS + REM
DEEP = 2 * MAIN + 128


def halves(value):
    high = value.astype(BF16)
    return high, (value - high.astype(F32)).astype(BF16)


def dot(a, b, dims):
    return lax.dot_general(a, b, dims, preferred_element_type=F32)


def product(a, b):
    a_high, a_low = halves(a)
    b_high, b_low = halves(b)
    return dot(a_high, b_high, NN) + dot(a_high, b_low, NN) + dot(a_low, b_high, NN)


def stacked(rows):
    high = rows.astype(BF16).astype(F32)
    return jnp.concatenate([high, rows - high], axis=0).astype(BF16)


def times_block(rows, block):
    both = stacked(rows)
    high, low = halves(block)
    out = dot(both, high, NT) + dot(both, low, NT)
    return out[:8] + out[8:]


def step(rows, weights):
    both = stacked(rows)
    main = both[:, :MAIN]
    out = (
        dot(main, weights[:, :MAIN], NT)
        + dot(main, weights[:, MAIN : 2 * MAIN], NT)
        + dot(both[:, MAIN:], weights[:, 2 * MAIN :], NT)
    )
    return out[:8] + out[8:]


def pack_weights(weights, matrix):
    high, low = halves(matrix)
    last = matrix[:, MAIN:]
    last_high = last.astype(BF16).astype(F32)
    tail = (
        last_high + pltpu.roll(last - last_high, REM, 1) + pltpu.roll(last_high, 2 * REM, 1)
    ).astype(BF16)
    for columns, values in (
        (slice(0, MAIN), high[:, :MAIN]),
        (slice(MAIN, 2 * MAIN), low[:, :MAIN]),
        (slice(2 * MAIN, DEEP), tail),
    ):
        weights[:ROWS, columns] = values[:ROWS]
        weights[ROWS:TWICE, columns] = values[MAIN:ROWS]
    weights[TWICE:, :] = jnp.zeros((WIDE - TWICE, DEEP), BF16)


def put_block(matrix, target, source, block):
    row, col = 128 * target, 128 * source
    row_rem, col_rem = MAIN + 8 * target, MAIN + 8 * source
    matrix[row : row + 128, col : col + 128] = block[:128, :128]
    matrix[row : row + 128, col_rem : col_rem + 7] = block[:128, 128:]
    matrix[row_rem : row_rem + 7, col : col + 128] = block[128:, :128]
    matrix[row_rem : row_rem + 7, col_rem : col_rem + 7] = block[128:, 128:]


def put_rows(packed, element, rows):
    packed[:, 128 * element : 128 * element + 128] = rows[:, :128]
    packed[:, MAIN + 8 * element : MAIN + 8 * element + 7] = rows[:, 128:]
    packed[:, ROWS + 8 * element : ROWS + 8 * element + 7] = rows[:, 128:]


def kernel(
    flows,
    crosses,
    color_ref,
    rhs_hbm,
    old_hbm,
    inv_hbm,
    faces_hbm,
    out_ref,
    rhs,
    old,
    inv,
    faces,
    halo_left,
    halo_right,
    below,
    own,
    other,
    weights,
    pair_weights,
    offset,
    other_offset,
    arrived,
    leaving,
    load_sem,
    send_sem,
    recv_sem,
):
    flow, cross = lax.axis_index("flow"), lax.axis_index("cross")
    core = lax.rem(flow, 2)
    odd = core == 1
    has_left, has_right = cross > 0, cross < crosses - 1
    has_upper, has_lower = flow > 0, flow < flows - 1

    def at(flow_step, cross_step):
        return (flow + flow_step, cross + cross_step)

    barrier = pltpu.get_barrier_semaphore()
    partners = [
        (has_upper, at(-1, 0)),
        (has_lower, at(1, 0)),
        (has_left, at(0, -1)),
        (has_right, at(0, 1)),
        (odd & (flow >= 2), at(-2, 0)),
        (odd & (flow < flows - 2), at(2, 0)),
    ]
    expected = 0
    for present, device in partners:
        expected = expected + present.astype(jnp.int32)

        @pl.when(present)
        def _(device=device):
            pl.semaphore_signal(barrier, inc=1, device_id=device, device_id_type=MESH)

    def block_load(place, face, j, k):
        source = inv_hbm.at[0] if face is None else faces_hbm.at[0, face]
        target = inv if face is None else faces.at[face]
        return pltpu.make_async_copy(
            source.at[j, :, k, :], target.at[j, k], load_sem.at[place]
        )

    wanted = [(face, j, k) for face in (None, 0, 2, 3) for j in (0, 1) for k in (0, 1)]
    wanted += [(4, j, 1) for j in (0, 1)] + [(5, j, 0) for j in (0, 1)]
    wanted += [(1, j, k) for j in (0, 1) for k in (0, 1)]
    loads = [block_load(place, *block) for place, block in enumerate(wanted)]
    loads += [
        pltpu.make_async_copy(old_hbm.at[0], old, load_sem.at[len(wanted)]),
        pltpu.make_async_copy(rhs_hbm.at[0], rhs, load_sem.at[len(wanted) + 1]),
    ]
    for load in loads:
        load.start()

    own[...] = jnp.zeros_like(own)
    offset[...] = jnp.zeros_like(offset)
    pl.semaphore_wait(barrier, expected)

    def remote(source, target, place, device):
        return pltpu.make_async_remote_copy(
            src_ref=source,
            dst_ref=target,
            send_sem=send_sem.at[place],
            recv_sem=recv_sem.at[place],
            device_id=device,
            device_id_type=MESH,
        )

    halos = [
        (has_right, has_left, remote(old_hbm.at[0, 1], halo_left, 0, at(0, 1))),
        (has_left, has_right, remote(old_hbm.at[0, 0], halo_right, 1, at(0, -1))),
        (has_upper, has_lower, remote(old_hbm.at[0], below, 2, at(-1, 0))),
    ]
    for sends, _, halo in halos:
        pl.when(sends)(halo.start)

    even = color_ref[0, 0, 0] == 0

    def pick(first, second):
        return jnp.where(even, first, second)

    def cross_face(e):
        return faces[3 - e // 2, e // 2, e % 2]

    def span_face(e):
        return faces[5 - e % 2, e // 2, e % 2]

    def out_face(e):
        return faces[2 + e // 2, e // 2, e % 2]

    def inverse(e):
        return inv[e // 2, e % 2]

    for load in loads:
        load.wait()

    matrix = [
        remote(own.at[rows], other.at[rows], place, at(1, 0))
        for place, rows in (
            (3, pl.ds(0, 256)),
            (4, pl.ds(256, 256)),
            (5, pl.ds(MAIN, REM)),
        )
    ]

    @pl.when(has_upper)
    def _():
        diagonal = [-product(inverse(e), faces[0, e // 2, e % 2]) for e in range(4)]
        for e in range(4):
            put_block(own, e, e, diagonal[e])
        from_a, from_d = pick(diagonal[0], diagonal[1]), pick(diagonal[3], diagonal[2])
        inv_b, inv_c = pick(inverse(1), inverse(0)), pick(inverse(2), inverse(3))
        gain_bd = product(inv_b, pick(cross_face(1), cross_face(0)))
        gain_ba = product(inv_b, pick(span_face(1), span_face(0)))
        gain_ca = product(inv_c, pick(cross_face(2), cross_face(3)))
        gain_cd = product(inv_c, pick(span_face(2), span_face(3)))
        for source, gain, here, there in (
            (from_a, gain_ba, (1, 0), (0, 1)),
            (from_d, gain_bd, (1, 3), (0, 2)),
            (from_a, gain_ca, (2, 0), (3, 1)),
            (from_d, gain_cd, (2, 3), (3, 2)),
        ):
            block = -product(gain, source)
            nothing = jnp.zeros_like(block)
            put_block(own, *here, pick(block, nothing))
            put_block(own, *there, pick(nothing, block))

        @pl.when(core == 0)
        def _():
            for piece in matrix:
                piece.start()

        pack_weights(weights, own[...])

    for _, receives, halo in halos:
        pl.when(receives)(halo.wait_recv)

    def part(e):
        j, k = e // 2, e % 2
        halo = jnp.where(*((has_left, halo_left[k]) if j == 0 else (has_right, halo_right[k])), 0.0)
        under = jnp.where(has_lower, below[j, k], 0.0)
        return (
            rhs[j, k]
            - times_block(under, faces[1, j, k])
            - times_block(halo, out_face(e))
        )

    parts = [part(e) for e in range(4)]
    held = [old[e // 2, e % 2] for e in range(4)]
    old_b, old_c = pick(held[1], held[0]), pick(held[2], held[3])
    total_a = pick(parts[0], parts[1]) - (
        times_block(old_c, pick(cross_face(0), cross_face(1)))
        + times_block(old_b, pick(span_face(0), span_face(1)))
    )
    total_d = pick(parts[3], parts[2]) - (
        times_block(old_b, pick(cross_face(3), cross_face(2)))
        + times_block(old_c, pick(span_face(3), span_face(2)))
    )
    new_a = times_block(total_a, pick(inverse(0), inverse(1)))
    new_d = times_block(total_d, pick(inverse(3), inverse(2)))
    total_b = pick(parts[1], parts[0]) - (
        times_block(new_d, pick(cross_face(1), cross_face(0)))
        + times_block(new_a, pick(span_face(1), span_face(0)))
    )
    total_c = pick(parts[2], parts[3]) - (
        times_block(new_a, pick(cross_face(2), cross_face(3)))
        + times_block(new_d, pick(span_face(2), span_face(3)))
    )
    new_b = times_block(total_b, pick(inverse(1), inverse(0)))
    new_c = times_block(total_c, pick(inverse(2), inverse(3)))
    put_rows(offset, 0, pick(new_a, new_b))
    put_rows(offset, 1, pick(new_b, new_a))
    put_rows(offset, 2, pick(new_c, new_d))
    put_rows(offset, 3, pick(new_d, new_c))

    offset_copy = remote(offset, other_offset, 6, at(1, 0))
    to_other = remote(leaving, arrived, 7, at(1, 0))
    to_next = remote(leaving, arrived, 8, at(2, 0))

    def finish(rows):
        for e in range(4):
            out_ref[0, e // 2, e % 2, :, :128] = rows[:, 128 * e : 128 * e + 128]
            out_ref[0, e // 2, e % 2, :, 128:] = rows[:, MAIN + 8 * e : MAIN + 8 * e + 7]

    @pl.when(core == 0)
    def _():
        offset_copy.start()

        @pl.when(flow == 0)
        def _():
            finish(offset[...])

        @pl.when(has_upper)
        def _():
            to_other.wait_recv()
            finish(step(arrived[...], weights[...]) + offset[...])
            for piece in matrix:
                piece.wait_send()

        offset_copy.wait_send()

    @pl.when(odd)
    def _():
        @pl.when(flow == 1)
        def _():
            offset_copy.wait_recv()
            leaving[...] = step(other_offset[...], weights[...]) + offset[...]

        @pl.when(flow > 1)
        def _():
            left = weights.at[:TWICE]
            paired = jnp.zeros((TWICE, WIDE), F32)
            for half in (0, 1):
                matrix[half].wait_recv()
                here = slice(256 * half, 256 * half + 256)
                low_here = slice(MAIN + 256 * half, MAIN + 256 * half + 256)
                high, low = halves(other[here, :])
                paired = (
                    paired
                    + dot(left[:, here], high, NN)
                    + dot(left[:, here], low, NN)
                    + dot(left[:, low_here], high, NN)
                )
            matrix[2].wait_recv()
            high, low = halves(other[MAIN:, :])
            tail = jnp.concatenate([high, high, low, jnp.zeros_like(high)], axis=0)
            paired = paired + dot(left[:, 2 * MAIN :], tail, NN)
            pack_weights(pair_weights, paired)
            offset_copy.wait_recv()
            offset[...] = step(other_offset[...], weights[...]) + offset[...]
            to_next.wait_recv()
            leaving[...] = step(arrived[...], pair_weights[...]) + offset[...]

        @pl.when(has_lower)
        def _():
            to_next.start()
            to_other.start()

        finish(leaving[...])

        @pl.when(has_lower)
        def _():
            to_next.wait_send()
            to_other.wait_send()

    for sends, _, halo in halos:
        pl.when(sends)(halo.wait_send)


def body(flows, crosses, right_side, start_iterate, inverse_blocks, face_blocks, color_order):
    _, columns, spans, vectors, width = right_side.shape
    hbm = pl.BlockSpec(memory_space=pltpu.HBM)
    return pl.pallas_call(
        functools.partial(kernel, flows, crosses),
        out_shape=jax.ShapeDtypeStruct(right_side.shape, F32),
        in_specs=[pl.BlockSpec(memory_space=pltpu.SMEM), hbm, hbm, hbm, hbm],
        out_specs=pl.BlockSpec(memory_space=pltpu.VMEM),
        scratch_shapes=[
            pltpu.VMEM((columns, spans, vectors, width), F32),
            pltpu.VMEM((columns, spans, vectors, width), F32),
            pltpu.VMEM((columns, spans, width, width), F32),
            pltpu.VMEM((6, columns, spans, width, width), F32),
            pltpu.VMEM((spans, vectors, width), F32),
            pltpu.VMEM((spans, vectors, width), F32),
            pltpu.VMEM((columns, spans, vectors, width), F32),
            pltpu.VMEM((ROWS, WIDE), F32),
            pltpu.VMEM((ROWS, WIDE), F32),
            pltpu.VMEM((WIDE, DEEP), BF16),
            pltpu.VMEM((WIDE, DEEP), BF16),
            pltpu.VMEM((vectors, WIDE), F32),
            pltpu.VMEM((vectors, WIDE), F32),
            pltpu.VMEM((vectors, WIDE), F32),
            pltpu.VMEM((vectors, WIDE), F32),
            pltpu.SemaphoreType.DMA((26,)),
            pltpu.SemaphoreType.DMA((9,)),
            pltpu.SemaphoreType.DMA((9,)),
        ],
        compiler_params=pltpu.CompilerParams(
            collective_id=0, has_side_effects=True, vmem_limit_bytes=60 * 1024 * 1024
        ),
        cost_estimate=pl.CostEstimate(flops=10**9, bytes_accessed=4 * 10**6, transcendentals=0),
        name="sweep_chain",
    )(
        color_order,
        right_side,
        start_iterate,
        inverse_blocks.transpose(0, 1, 3, 2, 4),
        face_blocks.transpose(0, 1, 2, 4, 3, 5),
    )


def solution(mesh):
    return jax.shard_map(
        functools.partial(body, mesh.shape["flow"], mesh.shape["cross"]),
        mesh=mesh,
        in_specs=(
            P("flow", "cross", None, None, None),
            P("flow", "cross", None, None, None),
            P("flow", "cross", None, None, None),
            P("flow", None, "cross", None, None, None),
            P("flow", "cross", None),
        ),
        out_specs=P("flow", "cross", None, None, None),
        check_vma=False,
    )
```

time: 271 us -> 51.8 us (0.19); the launches traced: 266 us -> 51.6 us
  waiting for transfers between devices: 103 us -> 0 us
  matrix products: 101 us -> 0 us
  Pallas kernels: 0 us -> 50.2 us
  blocking collectives: 27.5 us -> 0 us
  between operations: 13.7 us -> 0.01 us
  local copies, waits for them, and re-layouts: 11 us -> 1.38 us
  starting transfers between devices: 9.13 us -> 0 us
    all_gather x1 -> x0, waiting for transfers between devices: 103 us -> none  [prefix_2(): gathered = jax.tree.map(lambda a: lax.all_gather(a, axis), part)]
    dot_general x61 -> x0, matrix products: 101 us -> none  [the longest x30 67.8 us: compose(): jnp.dot(earlier[1], later[0], precision=lax.Precision.HIGHEST) + later[1]]
    pallas_call x0 -> x1, Pallas kernels: none -> 50.2 us  [body(): pl.pallas_call(functools.partial(kernel, flows, crosses), out_shape=jax.S...]
    all_gather x1 -> x0, blocking collectives: 27.5 us -> none  [prefix_2(): gathered = jax.tree.map(lambda a: lax.all_gather(a, axis), part)]
    ppermute x3 -> x0, starting transfers between devices: 9.13 us -> none  [the longest x1 5.02 us: with_halo(): lax.ppermute(tail, axis, [(i, (i + 1) % count) for i in range(ends)])]
    another operation x3 -> x0, local copies, waits for them, and re-layouts: 6.21 us -> none  [prefix_2(): gathered = jax.tree.map(lambda a: lax.all_gather(a, axis), part)]
    slice x5 -> x0, local copies, waits for them, and re-layouts: 3.14 us -> none  [the longest x1 3.02 us: layer(): faces[0]]
  transfers between devices with their start and end apart: 4 -> 0, of which waited for: 1 -> 0; matrix products, arithmetic and copies ran while one was open for 3% -> 0% of each run, Pallas kernels for 0% -> 0%
where the time goes in v1:
time: 51.8 us; the launch traced here: 51.6 us
  Pallas kernels  50.2 us (97%)
  local copies, waits for them, and re-layouts  1.38 us (3%)
    pallas_call x1, Pallas kernels, body(): pl.pallas_call(functools.partial(kernel, flows, crosses), out_shape=jax.S...  50.2 us
    unnamed x1, local copies, waits for them, and re-layouts  1.38 us

profile of v1, /device:TPU:126, one launch (start us, length us, event | category | flops | bytes accessed | tf_op | source)
XLA Modules:
  0.0 51.6 jit_solution(15326445585991536747)
XLA Ops:
  0.0 50.2 %sweep_chain.1 = f32[1,2,2,8,135]{4,3,2,1,0:T(8,128)} custom-call(s32[1,2,2]{2,1,0:T(2,128)} %color_ref.1, f32[1,2,2,8,135]{4,3,2,1,0:T(8,128)} %rhs_hbm.1, f32[1,2,2,8,135]{4,3,2,1,0:T(8,128)} %old_hbm.1, f32[1,2,135,2,135]{4,3,2,1,0:T(2,128)} %bitcast.3, f32[1,6,2,135,2,135]{5,4,3,2,1,0:T(2,128)} %bitcast.2), custom_call_target="tpu_custom_call" | custom-call | flops 1000000000 | bytes 4000000 | tf_op jit(solution)/shard_map/sweep_chain/pallas_call | solution.py:362
  50.2 1.4 %copy.7 = f32[1,2,2,8,135]{4,3,2,1,0:T(8,128)} copy(f32[1,2,2,8,135]{4,3,2,1,0:T(8,128)} %sweep_chain.1) | data formatting | bytes 34560

commit v2 on v1

v2 whole, which is shorter than its diff:
```python
import functools

import jax
import jax.numpy as jnp
from jax import lax
from jax.experimental import pallas as pl
from jax.experimental.pallas import tpu as pltpu
from jax.sharding import PartitionSpec as P

MESH = pl.DeviceIdType.MESH
BF16 = jnp.bfloat16
F32 = jnp.float32
NN = (((1,), (0,)), ((), ()))
NT = (((1,), (1,)), ((), ()))

MAIN, REM, WIDE = 512, 32, 640
ROWS = MAIN + REM
TWICE = ROWS + REM
DEEP = 2 * MAIN + 128
EDGE, SIDE, FLAG, SENT = 1024, 1088, 1224, 1232
OWN, FIRST, CHIP, FAR, FAR_NEXT, SOME, ALL = range(7)
PLACES = (
    ((0, 2), (None, 4), (None, 5), None),
    ((4, None), (2, 0), None, (5, None)),
    ((6, None), None, (3, 1), (7, None)),
    (None, (None, 6), (None, 7), (1, 3)),
)


def halves(value):
    high = value.astype(BF16)
    return high, (value - high.astype(F32)).astype(BF16)


def dot(a, b, dims):
    return lax.dot_general(a, b, dims, preferred_element_type=F32)


def product(a, b):
    a_high, a_low = halves(a)
    b_high, b_low = halves(b)
    return dot(a_high, b_high, NN) + dot(a_high, b_low, NN) + dot(a_low, b_high, NN)


def stacked(rows):
    high = rows.astype(BF16).astype(F32)
    return jnp.concatenate([high, rows - high], axis=0).astype(BF16)


def times_block(rows, block):
    both = stacked(rows)
    high, low = halves(block)
    out = dot(both, high, NT) + dot(both, low, NT)
    return out[:8] + out[8:]


def step(rows, weights):
    both = stacked(rows)
    main = both[:, :MAIN]
    out = (
        dot(main, weights[:, :MAIN], NT)
        + dot(main, weights[:, MAIN : 2 * MAIN], NT)
        + dot(both[:, MAIN:], weights[:, 2 * MAIN :], NT)
    )
    return out[:8] + out[8:]


def fast_step(rows, weights):
    both = stacked(rows)
    main = both[:, :MAIN]
    out = (
        dot(main, weights[:MAIN], NN)
        + dot(main, weights[MAIN : 2 * MAIN], NN)
        + dot(both[:, MAIN:], weights[2 * MAIN :], NN)
    )
    return out[:8] + out[8:]


def pack_turned(weights, matrix):
    high, low = halves(matrix.T)
    weights[:MAIN] = high[:MAIN]
    weights[MAIN : 2 * MAIN] = low[:MAIN]
    weights[2 * MAIN : 2 * MAIN + REM] = high[MAIN:ROWS]
    weights[2 * MAIN + REM : 2 * MAIN + 2 * REM] = low[MAIN:ROWS]
    weights[2 * MAIN + 2 * REM :] = jnp.zeros((128 - 2 * REM, WIDE), BF16)


def pack_weights(weights, matrix):
    high, low = halves(matrix)
    last = matrix[:, MAIN:]
    last_high = last.astype(BF16).astype(F32)
    tail = (
        last_high + pltpu.roll(last - last_high, REM, 1) + pltpu.roll(last_high, 2 * REM, 1)
    ).astype(BF16)
    for columns, values in (
        (slice(0, MAIN), high[:, :MAIN]),
        (slice(MAIN, 2 * MAIN), low[:, :MAIN]),
        (slice(2 * MAIN, DEEP), tail),
    ):
        weights[:ROWS, columns] = values[:ROWS]
        weights[ROWS:TWICE, columns] = values[MAIN:ROWS]
    weights[TWICE:, :] = jnp.zeros((WIDE - TWICE, DEEP), BF16)


def composed(weights, later, earlier):
    pack_weights(weights, later)
    high, low = halves(earlier)
    tail_high, tail_low = high[MAIN:ROWS], low[MAIN:ROWS]
    tail = jnp.concatenate([tail_high, tail_high, tail_low, jnp.zeros_like(tail_high)], axis=0)
    return (
        dot(weights[:, :MAIN], high[:MAIN], NN)
        + dot(weights[:, :MAIN], low[:MAIN], NN)
        + dot(weights[:, MAIN : 2 * MAIN], high[:MAIN], NN)
        + dot(weights[:, 2 * MAIN :], tail, NN)
    )


def put_block(sent, place, block):
    sent[128 * place : 128 * place + 128] = block[:128, :128]
    sent[EDGE + 8 * place : EDGE + 8 * place + 7] = block[128:, :128]


def put_side(sent, target, source, block):
    lane = 32 * target + 8 * source
    sent[SIDE : SIDE + 135, lane : lane + 7] = block[:, 128:]


def spread(matrix, sent):
    even = sent[FLAG : FLAG + 1] > 0.5
    lanes = lax.broadcasted_iota(jnp.int32, (1, 128), 1)

    def fetch(places, start, height):
        if places is None:
            return jnp.zeros((height, 128), F32)
        first, second = (
            0.0 if place is None else sent[start + height * place : start + height * place + height]
            for place in places
        )
        return jnp.where(even, first, second)

    side = sent[SIDE:FLAG]
    for target, row in enumerate(PLACES):
        top, edge = slice(128 * target, 128 * target + 128), slice(MAIN + 8 * target, MAIN + 8 * target + 8)
        for source, places in enumerate(row):
            columns = slice(128 * source, 128 * source + 128)
            matrix[top, columns] = fetch(places, 0, 128)
            matrix[edge, columns] = fetch(places, EDGE, 8)
        turned = side if target == 0 else pltpu.roll(side, 128 - 32 * target, 1)
        turned = jnp.where(lanes < REM, turned, 0.0)
        matrix[top, MAIN:] = turned[:128]
        matrix[edge, MAIN:] = turned[128:]


def put_rows(packed, element, rows):
    packed[:, 128 * element : 128 * element + 128] = rows[:, :128]
    packed[:, MAIN + 8 * element : MAIN + 8 * element + 7] = rows[:, 128:]
    packed[:, ROWS + 8 * element : ROWS + 8 * element + 7] = rows[:, 128:]


def kernel(
    flows,
    crosses,
    color_ref,
    rhs_hbm,
    old_hbm,
    inv_hbm,
    faces_hbm,
    out_ref,
    rhs,
    old,
    inv,
    faces,
    halo_left,
    halo_right,
    below,
    sent,
    got,
    matrices,
    offsets,
    parts,
    weights,
    turned,
    arrived,
    leaving,
    load_sem,
    send_sem,
    recv_sem,
    order_sem,
):
    flow, cross = lax.axis_index("flow"), lax.axis_index("cross")
    core = lax.rem(flow, 2)
    odd = core == 1
    has_left, has_right = cross > 0, cross < crosses - 1
    has_upper, has_lower = flow > 0, flow < flows - 1
    inner = flow > 1

    def among(*layers):
        return functools.reduce(jnp.logical_or, [flow == layer for layer in layers])

    before, after = among(15, 19, 27, 30, 31), among(11, 21)
    one_more, two_more = among(11, 15), among(19, 21, 27, 30, 31)
    express = after
    helper = among(12, 13, 16, 17, 22, 23, 24, 25, 28, 29)
    goes_first, signals = among(12, 13, 17, 22, 25, 29), among(17, 22, 25, 29)
    goes_after = among(16, 23, 24, 28)
    to_site_step = jnp.where(
        among(12, 22), -1, jnp.where(flow == 23, -2, jnp.where(among(13, 17, 25, 29), 2, 3))
    )

    def at(flow_step, cross_step):
        return (flow + flow_step, cross + cross_step)

    barrier = pltpu.get_barrier_semaphore()
    partners = [
        (has_upper, at(-1, 0)),
        (has_lower, at(1, 0)),
        (has_left, at(0, -1)),
        (has_right, at(0, 1)),
        (odd & (flow >= 2), at(-2, 0)),
        (odd & (flow < flows - 2), at(2, 0)),
    ]
    for distance, layers in ((3, (16, 21, 24, 27, 28)), (4, (11, 15, 21, 27)), (6, (21,))):
        partners.append((among(*layers), at(distance, 0)))
        partners.append((among(*(layer + distance for layer in layers)), at(-distance, 0)))
    expected = 0
    for present, device in partners:
        expected = expected + present.astype(jnp.int32)

        @pl.when(present)
        def _(device=device):
            pl.semaphore_signal(barrier, inc=1, device_id=device, device_id_type=MESH)

    def block_load(place, face, j, k):
        source = inv_hbm.at[0] if face is None else faces_hbm.at[0, face]
        target = inv if face is None else faces.at[face]
        return pltpu.make_async_copy(
            source.at[j, :, k, :], target.at[j, k], load_sem.at[place]
        )

    cells = [(j, k) for j in (0, 1) for k in (0, 1)]
    span_blocks = [(4, 0, 1), (4, 1, 1), (5, 0, 0), (5, 1, 0)]
    groups = [
        [(None, *cell) for cell in cells],
        [(0, *cell) for cell in cells],
        span_blocks + [(face, *cell) for face in (2, 3) for cell in cells],
        [(1, *cell) for cell in cells],
    ]
    count, loads = 0, []
    for group in groups:
        loads.append([block_load(count + n, *block) for n, block in enumerate(group)])
        count += len(group)
    old_load = pltpu.make_async_copy(old_hbm.at[0], old, load_sem.at[count])
    rhs_load = pltpu.make_async_copy(rhs_hbm.at[0], rhs, load_sem.at[count + 1])
    old_load.start()
    rhs_load.start()

    @pl.when(inner)
    def _():
        for n in (0, 1, 2, 3):
            for load in loads[n]:
                load.start()

    @pl.when(~inner)
    def _():
        for n in (2, 3, 0, 1):
            for load in loads[n]:
                load.start()

    sent[...] = jnp.zeros_like(sent)
    offsets[OWN] = jnp.zeros((8, WIDE), F32)
    arrived[0] = jnp.zeros((8, WIDE), F32)
    for slot in (OWN, FIRST, FAR, FAR_NEXT):
        matrices[slot, ROWS:] = jnp.zeros((WIDE - ROWS, WIDE), F32)
    pl.semaphore_wait(barrier, expected)

    def remote(source, target, places, device):
        sending, receiving = places if isinstance(places, tuple) else (places, places)
        return pltpu.make_async_remote_copy(
            src_ref=source,
            dst_ref=target,
            send_sem=send_sem.at[sending],
            recv_sem=recv_sem.at[receiving],
            device_id=device,
            device_id_type=MESH,
        )

    halos = [
        (has_right, has_left, remote(old_hbm.at[0, 1], halo_left, 0, at(0, 1))),
        (has_left, has_right, remote(old_hbm.at[0, 0], halo_right, 1, at(0, -1))),
        (has_upper, has_lower, remote(old_hbm.at[0], below, 2, at(-1, 0))),
    ]
    for sends, _, halo in halos:
        pl.when(sends)(halo.start)

    even = color_ref[0, 0, 0] == 0

    def pick(first, second):
        return jnp.where(even, first, second)

    def cross_face(e):
        return faces[3 - e // 2, e // 2, e % 2]

    def span_face(e):
        return faces[5 - e % 2, e // 2, e % 2]

    def out_face(e):
        return faces[2 + e // 2, e // 2, e % 2]

    def inverse(e):
        return inv[e // 2, e % 2]

    for n in (0, 2):
        for load in loads[n]:
            load.wait()

    to_second = remote(sent, got.at[0], 3, at(1, 0))
    to_site = remote(sent, got.at[1 + core], 4 + core, at(to_site_step, 0))
    @pl.when(inner)
    def _():
        for load in loads[1]:
            load.wait()
        diagonal = [-product(inverse(e), faces[0, e // 2, e % 2]) for e in range(4)]
        from_a, from_d = pick(diagonal[0], diagonal[1]), pick(diagonal[3], diagonal[2])
        put_block(sent, 0, from_a)
        put_block(sent, 1, from_d)
        put_block(sent, 2, pick(diagonal[1], diagonal[0]))
        put_block(sent, 3, pick(diagonal[2], diagonal[3]))
        for e in range(4):
            put_side(sent, e, e, diagonal[e])
        inv_b, inv_c = pick(inverse(1), inverse(0)), pick(inverse(2), inverse(3))
        gain_ba = product(inv_b, pick(span_face(1), span_face(0)))
        gain_bd = product(inv_b, pick(cross_face(1), cross_face(0)))
        gain_ca = product(inv_c, pick(cross_face(2), cross_face(3)))
        gain_cd = product(inv_c, pick(span_face(2), span_face(3)))
        for slot, source, gain, here, there in (
            (4, from_a, gain_ba, (1, 0), (0, 1)),
            (5, from_d, gain_bd, (1, 3), (0, 2)),
            (6, from_a, gain_ca, (2, 0), (3, 1)),
            (7, from_d, gain_cd, (2, 3), (3, 2)),
        ):
            block = -product(gain, source)
            nothing = jnp.zeros_like(block)
            put_block(sent, slot, block)
            put_side(sent, *here, pick(block, nothing))
            put_side(sent, *there, pick(nothing, block))
        sent[FLAG:] = jnp.where(even, 1.0, 0.0) + jnp.zeros((8, 128), F32)
        pl.when(~odd)(to_second.start)
        pl.when(goes_first)(to_site.start)
        spread(matrices.at[OWN], sent)

    old_load.wait()
    rhs_load.wait()
    held = [old[e // 2, e % 2] for e in range(4)]
    old_b, old_c = pick(held[1], held[0]), pick(held[2], held[3])
    around_a = times_block(old_c, pick(cross_face(0), cross_face(1))) + times_block(
        old_b, pick(span_face(0), span_face(1))
    )
    around_d = times_block(old_b, pick(cross_face(3), cross_face(2))) + times_block(
        old_c, pick(span_face(3), span_face(2))
    )

    for load in loads[3]:
        load.wait()
    for _, receives, halo in halos:
        pl.when(receives)(halo.wait_recv)

    def part(e):
        j, k = e // 2, e % 2
        halo = jnp.where(*((has_left, halo_left[k]) if j == 0 else (has_right, halo_right[k])), 0.0)
        under = jnp.where(has_lower, below[j, k], 0.0)
        return (
            rhs[j, k]
            - times_block(under, faces[1, j, k])
            - times_block(halo, out_face(e))
        )

    for e in range(4):
        parts[e] = part(e)

    own_offset, first_offset = offsets.at[OWN], offsets.at[FIRST]
    offset_to_second = remote(own_offset, first_offset, 6, at(1, 0))
    offset_to_site = remote(own_offset, offsets.at[FAR + core], 7 + core, at(to_site_step, 0))

    @pl.when(flow == 1)
    def _():
        for load in loads[1]:
            load.wait()
        offset_to_second.wait_recv()
        for e in range(4):
            upper = jnp.concatenate(
                [
                    first_offset[:, 128 * e : 128 * e + 128],
                    first_offset[:, MAIN + 8 * e : MAIN + 8 * e + 7],
                ],
                axis=1,
            )
            parts[e] = parts[e] - times_block(upper, faces[0, e // 2, e % 2])

    total_a = pick(parts[0], parts[1]) - around_a
    total_d = pick(parts[3], parts[2]) - around_d
    new_a = times_block(total_a, pick(inverse(0), inverse(1)))
    new_d = times_block(total_d, pick(inverse(3), inverse(2)))
    total_b = pick(parts[1], parts[0]) - (
        times_block(new_d, pick(cross_face(1), cross_face(0)))
        + times_block(new_a, pick(span_face(1), span_face(0)))
    )
    total_c = pick(parts[2], parts[3]) - (
        times_block(new_a, pick(cross_face(2), cross_face(3)))
        + times_block(new_d, pick(span_face(2), span_face(3)))
    )
    new_b = times_block(total_b, pick(inverse(1), inverse(0)))
    new_c = times_block(total_c, pick(inverse(2), inverse(3)))
    put_rows(own_offset, 0, pick(new_a, new_b))
    put_rows(own_offset, 1, pick(new_b, new_a))
    put_rows(own_offset, 2, pick(new_c, new_d))
    put_rows(own_offset, 3, pick(new_d, new_c))

    pl.when(~odd)(offset_to_second.start)
    pl.when(helper)(offset_to_site.start)

    @pl.when(signals)
    def _():
        to_site.wait_send()
        pl.semaphore_signal(
            order_sem, inc=1, device_id=at(1 - 2 * core, 0), device_id_type=MESH
        )

    @pl.when(goes_after)
    def _():
        pl.semaphore_wait(order_sem, 1)
        to_site.start()

    def state(slot, send_place, flow_step):
        return remote(leaving.at[slot], arrived.at[1], (send_place, 9), at(flow_step, 0))

    sends = [
        (among(15, 27), state(1, 9, 4)),
        (flow == 27, state(1, 10, 3)),
        (odd & ~among(13, 17, 23, 25, 29, 31), state(1, 11, 2)),
        (odd & ~among(23, 29, 31), state(1, 12, 1)),
    ]
    express_sends = [
        (flow == 21, state(0, 13, 6)),
        (among(11, 21), state(0, 14, 4)),
        (flow == 21, state(0, 15, 3)),
    ]
    receives_state = sends[0][1].wait_recv

    def passed(box):
        return [
            remote(got.at[box], got.at[box], (15 + box, 3 + box), at(-1, 0)),
            remote(offsets.at[2 + box], offsets.at[2 + box], (17 + box, 6 + box), at(-1, 0)),
        ]

    @pl.when(~inner)
    def _():
        leaving[1] = own_offset[...]
        for present, copy in sends:
            pl.when(present)(copy.start)

    @pl.when(inner)
    def _():
        def compose(turn, carry):
            box = jnp.where(turn == 0, 0, jnp.where(after, turn, 3 - turn))
            layer = jnp.where(turn == 0, FIRST, 2 + box)
            held = jnp.where(turn == 0, OWN, jnp.where(turn == 1, jnp.where(odd, CHIP, OWN), SOME))
            result = jnp.where(turn == 0, CHIP, jnp.where(turn == 1, SOME, ALL))
            held_later = (turn == 0) | before
            later = jnp.where(held_later, held, layer)
            earlier = jnp.where(held_later, layer, held)
            remote(sent, got.at[box], (3, 3 + box), at(-1, 0)).wait_recv()
            remote(own_offset, offsets.at[layer], (6, 6 + box), at(-1, 0)).wait_recv()

            @pl.when((flow == flows - 1) & (turn > 0))
            def _():
                for copy in passed(box):
                    copy.start()

            spread(matrices.at[layer], got.at[box])
            matrices[result] = composed(weights, matrices[later], matrices[earlier])
            offsets[result] = step(offsets[earlier], weights[...]) + offsets[later]
            return carry

        more = jnp.where(two_more, 2, jnp.where(one_more, 1, 0))
        lax.fori_loop(1 - core, 1 + more, compose, 0)

        used = jnp.where(two_more, ALL, jnp.where(one_more, SOME, jnp.where(odd, CHIP, OWN)))
        pack_turned(turned.at[0], matrices[used])

        @pl.when(express)
        def _():
            pack_turned(turned.at[1], matrices[CHIP])

        turns = jnp.where(express, 3, 2)

        def advance(turn, carry):
            pl.when(turn == 1)(receives_state)
            last = turn == turns - 1
            own = express & last
            rows = arrived[jnp.where(turn == 0, 0, 1)]
            moved = fast_step(rows, turned.at[jnp.where(own, 1, 0)])
            leaving[jnp.where(last, 1, 0)] = moved + offsets[jnp.where(own, CHIP, used)]

            @pl.when(express & (turn == 1))
            def _():
                for present, copy in express_sends:
                    pl.when(present)(copy.start)

            @pl.when(last)
            def _():
                for present, copy in sends:
                    pl.when(present)(copy.start)

            return carry

        lax.fori_loop(0, turns, advance, 0)

    rows = leaving[1]
    for e in range(4):
        out_ref[0, e // 2, e % 2, :, :128] = rows[:, 128 * e : 128 * e + 128]
        out_ref[0, e // 2, e % 2, :, 128:] = rows[:, MAIN + 8 * e : MAIN + 8 * e + 7]

    for present, copy in sends:
        pl.when(present)(copy.wait_send)

    for present, copy in express_sends:
        pl.when(present)(copy.wait_send)

    @pl.when(flow == flows - 1)
    def _():
        for box in (1, 2):
            for copy in passed(box):
                copy.wait_send()

    @pl.when(flow == 0)
    def _():
        for load in loads[1]:
            load.wait()

    pl.when(inner & ~odd)(to_second.wait_send)
    pl.when(~odd)(offset_to_second.wait_send)
    pl.when(helper & ~signals)(to_site.wait_send)
    pl.when(helper)(offset_to_site.wait_send)
    for sends, _, halo in halos:
        pl.when(sends)(halo.wait_send)


def body(flows, crosses, right_side, start_iterate, inverse_blocks, face_blocks, color_order):
    _, columns, spans, vectors, width = right_side.shape
    hbm = pl.BlockSpec(memory_space=pltpu.HBM)
    return pl.pallas_call(
        functools.partial(kernel, flows, crosses),
        out_shape=jax.ShapeDtypeStruct(right_side.shape, F32),
        in_specs=[pl.BlockSpec(memory_space=pltpu.SMEM), hbm, hbm, hbm, hbm],
        out_specs=pl.BlockSpec(memory_space=pltpu.VMEM),
        scratch_shapes=[
            pltpu.VMEM((columns, spans, vectors, width), F32),
            pltpu.VMEM((columns, spans, vectors, width), F32),
            pltpu.VMEM((columns, spans, width, width), F32),
            pltpu.VMEM((6, columns, spans, width, width), F32),
            pltpu.VMEM((spans, vectors, width), F32),
            pltpu.VMEM((spans, vectors, width), F32),
            pltpu.VMEM((columns, spans, vectors, width), F32),
            pltpu.VMEM((SENT, 128), F32),
            pltpu.VMEM((3, SENT, 128), F32),
            pltpu.VMEM((7, WIDE, WIDE), F32),
            pltpu.VMEM((7, vectors, WIDE), F32),
            pltpu.VMEM((2 * columns, vectors, width), F32),
            pltpu.VMEM((WIDE, DEEP), BF16),
            pltpu.VMEM((2, DEEP, WIDE), BF16),
            pltpu.VMEM((2, vectors, WIDE), F32),
            pltpu.VMEM((2, vectors, WIDE), F32),
            pltpu.SemaphoreType.DMA((26,)),
            pltpu.SemaphoreType.DMA((20,)),
            pltpu.SemaphoreType.DMA((10,)),
            pltpu.SemaphoreType.REGULAR,
        ],
        compiler_params=pltpu.CompilerParams(
            collective_id=0, has_side_effects=True, vmem_limit_bytes=60 * 1024 * 1024
        ),
        cost_estimate=pl.CostEstimate(flops=10**9, bytes_accessed=4 * 10**6, transcendentals=0),
        name="sweep_chain",
    )(
        color_order,
        right_side,
        start_iterate,
        inverse_blocks.transpose(0, 1, 3, 2, 4),
        face_blocks.transpose(0, 1, 2, 4, 3, 5),
    )


def solution(mesh):
    return jax.shard_map(
        functools.partial(body, mesh.shape["flow"], mesh.shape["cross"]),
        mesh=mesh,
        in_specs=(
            P("flow", "cross", None, None, None),
            P("flow", "cross", None, None, None),
            P("flow", "cross", None, None, None),
            P("flow", None, "cross", None, None, None),
            P("flow", "cross", None),
        ),
        out_specs=P("flow", "cross", None, None, None),
        check_vma=False,
    )
```

time: 51.8 us -> 40.2 us (0.78)
  the two profiles are of different devices: /device:TPU:126 before, /device:TPU:78 now
where the time goes in v2:
time: 40.2 us; the launch traced here: 40 us
  Pallas kernels  38.7 us (96%)
  local copies, waits for them, and re-layouts  1.38 us (3%)
    pallas_call x1, Pallas kernels, body(): pl.pallas_call(functools.partial(kernel, flows, crosses), out_shape=jax.S...  38.7 us
    unnamed x1, local copies, waits for them, and re-layouts  1.38 us

profile of v2, /device:TPU:78, one launch (start us, length us, event | category | flops | bytes accessed | tf_op | source)
XLA Modules:
  0.0 40.0 jit_solution(10566864305580665217)
XLA Ops:
  0.0 38.7 %sweep_chain.1 = f32[1,2,2,8,135]{4,3,2,1,0:T(8,128)} custom-call(s32[1,2,2]{2,1,0:T(2,128)} %color_ref.1, f32[1,2,2,8,135]{4,3,2,1,0:T(8,128)} %rhs_hbm.1, f32[1,2,2,8,135]{4,3,2,1,0:T(8,128)} %old_hbm.1, f32[1,2,135,2,135]{4,3,2,1,0:T(2,128)} %bitcast.3, f32[1,6,2,135,2,135]{5,4,3,2,1,0:T(2,128)} %bitcast.2), custom_call_target="tpu_custom_call" | custom-call | flops 1000000000 | bytes 4000000 | tf_op jit(solution)/shard_map/sweep_chain/pallas_call | solution.py:551
  38.7 1.4 %copy.7 = f32[1,2,2,8,135]{4,3,2,1,0:T(8,128)} copy(f32[1,2,2,8,135]{4,3,2,1,0:T(8,128)} %sweep_chain.1) | data formatting | bytes 34560

commit v3 on v2

--- a/solution.py
+++ b/solution.py
@@ -18,7 +18,8 @@
 TWICE = ROWS + REM
 DEEP = 2 * MAIN + 128
 EDGE, SIDE, FLAG, SENT = 1024, 1088, 1224, 1232
-OWN, FIRST, CHIP, FAR, FAR_NEXT, SOME, ALL = range(7)
+HALF = SENT // 2
+OWN, FIRST, CHIP, FAR, MORE = 0, 1, 2, 3, 5
 PLACES = (
     ((0, 2), (None, 4), (None, 5), None),
     ((4, None), (2, 0), None, (5, None)),
@@ -47,11 +48,14 @@
     return jnp.concatenate([high, rows - high], axis=0).astype(BF16)
 
 
-def times_block(rows, block):
+def times_halves(rows, high, low):
     both = stacked(rows)
-    high, low = halves(block)
     out = dot(both, high, NT) + dot(both, low, NT)
     return out[:8] + out[8:]
+
+
+def times_block(rows, block):
+    return times_halves(rows, *halves(block))
 
 
 def step(rows, weights):
@@ -178,6 +182,7 @@
     matrices,
     offsets,
     parts,
+    blocks,
     weights,
     turned,
     arrived,
@@ -197,15 +202,19 @@
     def among(*layers):
         return functools.reduce(jnp.logical_or, [flow == layer for layer in layers])
 
-    before, after = among(15, 19, 27, 30, 31), among(11, 21)
-    one_more, two_more = among(11, 15), among(19, 21, 27, 30, 31)
-    express = after
-    helper = among(12, 13, 16, 17, 22, 23, 24, 25, 28, 29)
-    goes_first, signals = among(12, 13, 17, 22, 25, 29), among(17, 22, 25, 29)
-    goes_after = among(16, 23, 24, 28)
+    before, express = among(19, 26, 27, 30, 31), among(9, 13, 21)
+    more = jnp.where(
+        flow == 9, 1, jnp.where(flow == 19, 3, jnp.where(among(13, 21, 26, 27, 30, 31), 2, 0))
+    )
+    passes = among(27, 31)
+    helper = among(10, 11, 14, 15, 16, 17, 22, 23, 24, 25, 28, 29)
+    signals, goes_after = among(14, 17, 22, 25, 29), among(15, 16, 23, 24, 28)
     to_site_step = jnp.where(
-        among(12, 22), -1, jnp.where(flow == 23, -2, jnp.where(among(13, 17, 25, 29), 2, 3))
-    )
+        among(10, 14, 22),
+        -1,
+        jnp.where(flow == 23, -2, jnp.where(flow == 15, 4, jnp.where(odd, 2, 3))),
+    )
+    to_site_box = jnp.where(flow == 15, 3, 1 + core)
 
     def at(flow_step, cross_step):
         return (flow + flow_step, cross + cross_step)
@@ -219,7 +228,12 @@
         (odd & (flow >= 2), at(-2, 0)),
         (odd & (flow < flows - 2), at(2, 0)),
     ]
-    for distance, layers in ((3, (16, 21, 24, 27, 28)), (4, (11, 15, 21, 27)), (6, (21,))):
+    for distance, layers in (
+        (3, (16, 21, 24, 27, 28)),
+        (4, (9, 15, 21, 27)),
+        (5, (21,)),
+        (6, (13, 21)),
+    ):
         partners.append((among(*layers), at(distance, 0)))
         partners.append((among(*(layer + distance for layer in layers)), at(-distance, 0)))
     expected = 0
@@ -269,7 +283,7 @@
     sent[...] = jnp.zeros_like(sent)
     offsets[OWN] = jnp.zeros((8, WIDE), F32)
     arrived[0] = jnp.zeros((8, WIDE), F32)
-    for slot in (OWN, FIRST, FAR, FAR_NEXT):
+    for slot in (OWN, FIRST, FAR, FAR + 1, FAR + 2):
         matrices[slot, ROWS:] = jnp.zeros((WIDE - ROWS, WIDE), F32)
     pl.semaphore_wait(barrier, expected)
 
@@ -313,8 +327,20 @@
         for load in loads[n]:
             load.wait()
 
-    to_second = remote(sent, got.at[0], 3, at(1, 0))
-    to_site = remote(sent, got.at[1 + core], 4 + core, at(to_site_step, 0))
+    def in_halves(source, target, places, box, flow_step):
+        return [
+            remote(
+                source.at[pl.ds(HALF * n, HALF)],
+                target.at[pl.ds(HALF * n, HALF)],
+                (places + n, (3, 12)[n] + box),
+                at(flow_step, 0),
+            )
+            for n in (0, 1)
+        ]
+
+    to_second = in_halves(sent, got.at[0], 3, 0, 1)
+    to_site = in_halves(sent, got.at[to_site_box], 5, to_site_box, to_site_step)
+
     @pl.when(inner)
     def _():
         for load in loads[1]:
@@ -344,9 +370,12 @@
             put_side(sent, *here, pick(block, nothing))
             put_side(sent, *there, pick(nothing, block))
         sent[FLAG:] = jnp.where(even, 1.0, 0.0) + jnp.zeros((8, 128), F32)
-        pl.when(~odd)(to_second.start)
-        pl.when(goes_first)(to_site.start)
+        for copy in to_second:
+            pl.when(~odd)(copy.start)
+        for copy in to_site:
+            pl.when(helper & ~goes_after)(copy.start)
         spread(matrices.at[OWN], sent)
+        matrices[OWN, ROWS:TWICE] = matrices[OWN, MAIN:ROWS]
 
     old_load.wait()
     rhs_load.wait()
@@ -361,6 +390,27 @@
 
     for load in loads[3]:
         load.wait()
+
+    for e in range(4):
+        blocks[2 * e, 0], blocks[2 * e, 1] = halves(faces[1, e // 2, e % 2])
+        blocks[2 * e + 1, 0], blocks[2 * e + 1, 1] = halves(out_face(e))
+    for n, block in enumerate(
+        (
+            pick(inverse(0), inverse(1)),
+            pick(inverse(3), inverse(2)),
+            pick(cross_face(1), cross_face(0)),
+            pick(span_face(1), span_face(0)),
+            pick(cross_face(2), cross_face(3)),
+            pick(span_face(2), span_face(3)),
+            pick(inverse(1), inverse(0)),
+            pick(inverse(2), inverse(3)),
+        )
+    ):
+        blocks[8 + n, 0], blocks[8 + n, 1] = halves(block)
+
+    def times(rows, n):
+        return times_halves(rows, blocks[n, 0], blocks[n, 1])
+
     for _, receives, halo in halos:
         pl.when(receives)(halo.wait_recv)
 
@@ -370,16 +420,18 @@
         under = jnp.where(has_lower, below[j, k], 0.0)
         return (
             rhs[j, k]
-            - times_block(under, faces[1, j, k])
-            - times_block(halo, out_face(e))
+            - times(under, 2 * e)
+            - times(halo, 2 * e + 1)
         )
 
     for e in range(4):
         parts[e] = part(e)
 
     own_offset, first_offset = offsets.at[OWN], offsets.at[FIRST]
-    offset_to_second = remote(own_offset, first_offset, 6, at(1, 0))
-    offset_to_site = remote(own_offset, offsets.at[FAR + core], 7 + core, at(to_site_step, 0))
+    offset_to_second = remote(own_offset, first_offset, (7, 7), at(1, 0))
+    offset_to_site = remote(
+        own_offset, offsets.at[2 + to_site_box], (8, 7 + to_site_box), at(to_site_step, 0)
+    )
 
     @pl.when(flow == 1)
     def _():
@@ -398,18 +450,10 @@
 
     total_a = pick(parts[0], parts[1]) - around_a
     total_d = pick(parts[3], parts[2]) - around_d
-    new_a = times_block(total_a, pick(inverse(0), inverse(1)))
-    new_d = times_block(total_d, pick(inverse(3), inverse(2)))
-    total_b = pick(parts[1], parts[0]) - (
-        times_block(new_d, pick(cross_face(1), cross_face(0)))
-        + times_block(new_a, pick(span_face(1), span_face(0)))
-    )
-    total_c = pick(parts[2], parts[3]) - (
-        times_block(new_a, pick(cross_face(2), cross_face(3)))
-        + times_block(new_d, pick(span_face(2), span_face(3)))
-    )
-    new_b = times_block(total_b, pick(inverse(1), inverse(0)))
-    new_c = times_block(total_c, pick(inverse(2), inverse(3)))
+    new_a, new_d = times(total_a, 8), times(total_d, 9)
+    total_b = pick(parts[1], parts[0]) - (times(new_d, 10) + times(new_a, 11))
+    total_c = pick(parts[2], parts[3]) - (times(new_a, 12) + times(new_d, 13))
+    new_b, new_c = times(total_b, 14), times(total_c, 15)
     put_rows(own_offset, 0, pick(new_a, new_b))
     put_rows(own_offset, 1, pick(new_b, new_a))
     put_rows(own_offset, 2, pick(new_c, new_d))
@@ -420,7 +464,7 @@
 
     @pl.when(signals)
     def _():
-        to_site.wait_send()
+        to_site[0].wait_send()
         pl.semaphore_signal(
             order_sem, inc=1, device_id=at(1 - 2 * core, 0), device_id_type=MESH
         )
@@ -428,29 +472,30 @@
     @pl.when(goes_after)
     def _():
         pl.semaphore_wait(order_sem, 1)
-        to_site.start()
+        for copy in to_site:
+            copy.start()
 
     def state(slot, send_place, flow_step):
-        return remote(leaving.at[slot], arrived.at[1], (send_place, 9), at(flow_step, 0))
+        return remote(leaving.at[slot], arrived.at[1], (send_place, 11), at(flow_step, 0))
 
     sends = [
-        (among(15, 27), state(1, 9, 4)),
+        (flow == 27, state(1, 9, 4)),
         (flow == 27, state(1, 10, 3)),
-        (odd & ~among(13, 17, 23, 25, 29, 31), state(1, 11, 2)),
-        (odd & ~among(23, 29, 31), state(1, 12, 1)),
+        (odd & ~among(11, 13, 17, 23, 25, 29, 31), state(1, 11, 2)),
+        (odd & ~among(23, 25, 29, 31), state(1, 12, 1)),
     ]
     express_sends = [
-        (flow == 21, state(0, 13, 6)),
-        (among(11, 21), state(0, 14, 4)),
-        (flow == 21, state(0, 15, 3)),
+        (among(13, 21), state(0, 13, 6)),
+        (flow == 21, state(0, 14, 5)),
+        (among(9, 21), state(0, 15, 4)),
+        (flow == 21, state(0, 16, 3)),
+        (flow == 13, state(0, 17, 2)),
     ]
     receives_state = sends[0][1].wait_recv
 
     def passed(box):
-        return [
-            remote(got.at[box], got.at[box], (15 + box, 3 + box), at(-1, 0)),
-            remote(offsets.at[2 + box], offsets.at[2 + box], (17 + box, 6 + box), at(-1, 0)),
-        ]
+        offset = remote(offsets.at[2 + box], offsets.at[2 + box], (17 + box, 7 + box), at(-1, 0))
+        return in_halves(got.at[box], got.at[box], 18 + 2 * box, box, -1) + [offset]
 
     @pl.when(~inner)
     def _():
@@ -460,18 +505,23 @@
 
     @pl.when(inner)
     def _():
+        base = jnp.where(odd, CHIP, OWN)
+
         def compose(turn, carry):
-            box = jnp.where(turn == 0, 0, jnp.where(after, turn, 3 - turn))
+            box = jnp.where(
+                (turn == 0) | (turn == 3) | among(9, 21), turn, 3 - turn
+            )
             layer = jnp.where(turn == 0, FIRST, 2 + box)
-            held = jnp.where(turn == 0, OWN, jnp.where(turn == 1, jnp.where(odd, CHIP, OWN), SOME))
-            result = jnp.where(turn == 0, CHIP, jnp.where(turn == 1, SOME, ALL))
-            held_later = (turn == 0) | before
+            held = jnp.where(turn == 0, OWN, jnp.where(turn == 1, base, MORE - 1 + turn))
+            result = jnp.where(turn == 0, CHIP, MORE + turn)
+            held_later = (turn == 0) | before | ((flow == 13) & (turn == 1))
             later = jnp.where(held_later, held, layer)
             earlier = jnp.where(held_later, layer, held)
-            remote(sent, got.at[box], (3, 3 + box), at(-1, 0)).wait_recv()
-            remote(own_offset, offsets.at[layer], (6, 6 + box), at(-1, 0)).wait_recv()
-
-            @pl.when((flow == flows - 1) & (turn > 0))
+            for copy in in_halves(sent, got.at[box], 3, box, -1):
+                copy.wait_recv()
+            remote(own_offset, offsets.at[layer], (7, 7 + box), at(-1, 0)).wait_recv()
+
+            @pl.when(passes & (turn > 0))
             def _():
                 for copy in passed(box):
                     copy.start()
@@ -481,15 +531,15 @@
             offsets[result] = step(offsets[earlier], weights[...]) + offsets[later]
             return carry
 
-        more = jnp.where(two_more, 2, jnp.where(one_more, 1, 0))
         lax.fori_loop(1 - core, 1 + more, compose, 0)
 
-        used = jnp.where(two_more, ALL, jnp.where(one_more, SOME, jnp.where(odd, CHIP, OWN)))
+        own_used = jnp.where(flow == 13, MORE + 1, CHIP)
+        used = jnp.where(more > 0, MORE + more, jnp.where(odd & (flow != 15), CHIP, OWN))
         pack_turned(turned.at[0], matrices[used])
 
         @pl.when(express)
         def _():
-            pack_turned(turned.at[1], matrices[CHIP])
+            pack_turned(turned.at[1], matrices[own_used])
 
         turns = jnp.where(express, 3, 2)
 
@@ -499,7 +549,7 @@
             own = express & last
             rows = arrived[jnp.where(turn == 0, 0, 1)]
             moved = fast_step(rows, turned.at[jnp.where(own, 1, 0)])
-            leaving[jnp.where(last, 1, 0)] = moved + offsets[jnp.where(own, CHIP, used)]
+            leaving[jnp.where(last, 1, 0)] = moved + offsets[jnp.where(own, own_used, used)]
 
             @pl.when(express & (turn == 1))
             def _():
@@ -526,7 +576,7 @@
     for present, copy in express_sends:
         pl.when(present)(copy.wait_send)
 
-    @pl.when(flow == flows - 1)
+    @pl.when(passes)
     def _():
         for box in (1, 2):
             for copy in passed(box):
@@ -537,9 +587,11 @@
         for load in loads[1]:
             load.wait()
 
-    pl.when(inner & ~odd)(to_second.wait_send)
+    for copy in to_second:
+        pl.when(inner & ~odd)(copy.wait_send)
     pl.when(~odd)(offset_to_second.wait_send)
-    pl.when(helper & ~signals)(to_site.wait_send)
+    pl.when(helper & ~signals)(to_site[0].wait_send)
+    pl.when(helper)(to_site[1].wait_send)
     pl.when(helper)(offset_to_site.wait_send)
     for sends, _, halo in halos:
         pl.when(sends)(halo.wait_send)
@@ -562,17 +614,18 @@
             pltpu.VMEM((spans, vectors, width), F32),
             pltpu.VMEM((columns, spans, vectors, width), F32),
             pltpu.VMEM((SENT, 128), F32),
-            pltpu.VMEM((3, SENT, 128), F32),
-            pltpu.VMEM((7, WIDE, WIDE), F32),
-            pltpu.VMEM((7, vectors, WIDE), F32),
+            pltpu.VMEM((4, SENT, 128), F32),
+            pltpu.VMEM((9, WIDE, WIDE), F32),
+            pltpu.VMEM((9, vectors, WIDE), F32),
             pltpu.VMEM((2 * columns, vectors, width), F32),
+            pltpu.VMEM((16, 2, width, width), BF16),
             pltpu.VMEM((WIDE, DEEP), BF16),
             pltpu.VMEM((2, DEEP, WIDE), BF16),
             pltpu.VMEM((2, vectors, WIDE), F32),
             pltpu.VMEM((2, vectors, WIDE), F32),
             pltpu.SemaphoreType.DMA((26,)),
-            pltpu.SemaphoreType.DMA((20,)),
-            pltpu.SemaphoreType.DMA((10,)),
+            pltpu.SemaphoreType.DMA((24,)),
+            pltpu.SemaphoreType.DMA((16,)),
             pltpu.SemaphoreType.REGULAR,
         ],
         compiler_params=pltpu.CompilerParams(

time: 40.2 us -> 41.4 us (1.030)
  the two profiles are of different devices: /device:TPU:78 before, /device:TPU:126 now
where the time goes in v3:
time: 41.4 us; the launch traced here: 41.2 us
  Pallas kernels  39.8 us (96%)
  local copies, waits for them, and re-layouts  1.38 us (3%)
    pallas_call x1, Pallas kernels, body(): pl.pallas_call(functools.partial(kernel, flows, crosses), out_shape=jax.S...  39.8 us
    unnamed x1, local copies, waits for them, and re-layouts  1.38 us

profile of v3, /device:TPU:126, one launch (start us, length us, event | category | flops | bytes accessed | tf_op | source)
XLA Modules:
  0.0 41.2 jit_solution(18042739649663399370)
XLA Ops:
  0.0 39.8 %sweep_chain.1 = f32[1,2,2,8,135]{4,3,2,1,0:T(8,128)} custom-call(s32[1,2,2]{2,1,0:T(2,128)} %color_ref.1, f32[1,2,2,8,135]{4,3,2,1,0:T(8,128)} %rhs_hbm.1, f32[1,2,2,8,135]{4,3,2,1,0:T(8,128)} %old_hbm.1, f32[1,2,135,2,135]{4,3,2,1,0:T(2,128)} %bitcast.3, f32[1,6,2,135,2,135]{5,4,3,2,1,0:T(2,128)} %bitcast.2), custom_call_target="tpu_custom_call" | custom-call | flops 1000000000 | bytes 4000000 | tf_op jit(solution)/shard_map/sweep_chain/pallas_call | solution.py:603
  39.9 1.4 %copy.7 = f32[1,2,2,8,135]{4,3,2,1,0:T(8,128)} copy(f32[1,2,2,8,135]{4,3,2,1,0:T(8,128)} %sweep_chain.1) | data formatting | bytes 34560

commit v4 on v3

--- a/solution.py
+++ b/solution.py
@@ -17,8 +17,9 @@
 ROWS = MAIN + REM
 TWICE = ROWS + REM
 DEEP = 2 * MAIN + 128
-EDGE, SIDE, FLAG, SENT = 1024, 1088, 1224, 1232
-HALF = SENT // 2
+EDGE, SIDE, FLAG, SENT = 1024, 1088, 1224, 1248
+PARTS = 4
+PART = SENT // PARTS
 OWN, FIRST, CHIP, FAR, MORE = 0, 1, 2, 3, 5
 PLACES = (
     ((0, 2), (None, 4), (None, 5), None),
@@ -204,16 +205,17 @@
 
     before, express = among(19, 26, 27, 30, 31), among(9, 13, 21)
     more = jnp.where(
-        flow == 9, 1, jnp.where(flow == 19, 3, jnp.where(among(13, 21, 26, 27, 30, 31), 2, 0))
+        flow == 9, 1, jnp.where(flow == 13, 3, jnp.where(among(19, 21, 26, 27, 30, 31), 2, 0))
     )
     passes = among(27, 31)
     helper = among(10, 11, 14, 15, 16, 17, 22, 23, 24, 25, 28, 29)
-    signals, goes_after = among(14, 17, 22, 25, 29), among(15, 16, 23, 24, 28)
+    signals, goes_after = among(22, 25, 29), among(23, 24, 28)
     to_site_step = jnp.where(
         among(10, 14, 22),
         -1,
-        jnp.where(flow == 23, -2, jnp.where(flow == 15, 4, jnp.where(odd, 2, 3))),
-    )
+        jnp.where(among(15, 23), -2, jnp.where(odd, 2, 3)),
+    )
+    relayed, relays = among(15, 16), among(4, 10)
     to_site_box = jnp.where(flow == 15, 3, 1 + core)
 
     def at(flow_step, cross_step):
@@ -229,10 +231,12 @@
         (odd & (flow < flows - 2), at(2, 0)),
     ]
     for distance, layers in (
-        (3, (16, 21, 24, 27, 28)),
-        (4, (9, 15, 21, 27)),
+        (3, (13, 16, 21, 24, 27, 28)),
+        (4, (9, 13, 21, 27)),
         (5, (21,)),
-        (6, (13, 21)),
+        (6, (10, 13, 21)),
+        (9, (4, 10)),
+        (11, (4,)),
     ):
         partners.append((among(*layers), at(distance, 0)))
         partners.append((among(*(layer + distance for layer in layers)), at(-distance, 0)))
@@ -323,28 +327,43 @@
     def inverse(e):
         return inv[e // 2, e % 2]
 
-    for n in (0, 2):
-        for load in loads[n]:
-            load.wait()
-
-    def in_halves(source, target, places, box, flow_step):
+    def in_parts(source, target, sending, receiving, flow_step):
         return [
             remote(
-                source.at[pl.ds(HALF * n, HALF)],
-                target.at[pl.ds(HALF * n, HALF)],
-                (places + n, (3, 12)[n] + box),
+                source.at[pl.ds(PART * n, PART)],
+                target.at[pl.ds(PART * n, PART)],
+                (sending + n, receiving + n),
                 at(flow_step, 0),
             )
-            for n in (0, 1)
+            for n in range(PARTS)
         ]
 
-    to_second = in_halves(sent, got.at[0], 3, 0, 1)
-    to_site = in_halves(sent, got.at[to_site_box], 5, to_site_box, to_site_step)
+    def received(box):
+        return 3 + PARTS * box
+
+    to_second = in_parts(sent, got.at[0], 3, received(0), 1)
+    to_site = in_parts(
+        sent,
+        got.at[jnp.where(relayed, 1, to_site_box)],
+        7,
+        jnp.where(relayed, 24, received(to_site_box)),
+        jnp.where(flow == 15, -11, jnp.where(flow == 16, -6, to_site_step)),
+    )
+    relay_box = jnp.where(flow == 4, 3, 1)
+    to_relay = in_parts(sent, got.at[1], 32, 24, -1)
+    relay = in_parts(got.at[1], got.at[relay_box], 32, received(relay_box), 9)
+
+    @pl.when(~inner)
+    def _():
+        for n in (0, 2):
+            for load in loads[n]:
+                load.wait()
 
     @pl.when(inner)
     def _():
-        for load in loads[1]:
-            load.wait()
+        for n in (0, 1):
+            for load in loads[n]:
+                load.wait()
         diagonal = [-product(inverse(e), faces[0, e // 2, e % 2]) for e in range(4)]
         from_a, from_d = pick(diagonal[0], diagonal[1]), pick(diagonal[3], diagonal[2])
         put_block(sent, 0, from_a)
@@ -353,6 +372,8 @@
         put_block(sent, 3, pick(diagonal[2], diagonal[3]))
         for e in range(4):
             put_side(sent, e, e, diagonal[e])
+        for load in loads[2]:
+            load.wait()
         inv_b, inv_c = pick(inverse(1), inverse(0)), pick(inverse(2), inverse(3))
         gain_ba = product(inv_b, pick(span_face(1), span_face(0)))
         gain_bd = product(inv_b, pick(cross_face(1), cross_face(0)))
@@ -369,11 +390,11 @@
             put_block(sent, slot, block)
             put_side(sent, *here, pick(block, nothing))
             put_side(sent, *there, pick(nothing, block))
-        sent[FLAG:] = jnp.where(even, 1.0, 0.0) + jnp.zeros((8, 128), F32)
+        sent[FLAG:] = jnp.where(even, 1.0, 0.0) + jnp.zeros((SENT - FLAG, 128), F32)
+        for copy in to_site:
+            pl.when(helper & ~goes_after)(copy.start)
         for copy in to_second:
             pl.when(~odd)(copy.start)
-        for copy in to_site:
-            pl.when(helper & ~goes_after)(copy.start)
         spread(matrices.at[OWN], sent)
         matrices[OWN, ROWS:TWICE] = matrices[OWN, MAIN:ROWS]
 
@@ -428,9 +449,9 @@
         parts[e] = part(e)
 
     own_offset, first_offset = offsets.at[OWN], offsets.at[FIRST]
-    offset_to_second = remote(own_offset, first_offset, (7, 7), at(1, 0))
+    offset_to_second = remote(own_offset, first_offset, (11, 19), at(1, 0))
     offset_to_site = remote(
-        own_offset, offsets.at[2 + to_site_box], (8, 7 + to_site_box), at(to_site_step, 0)
+        own_offset, offsets.at[2 + to_site_box], (12, 19 + to_site_box), at(to_site_step, 0)
     )
 
     @pl.when(flow == 1)
@@ -464,7 +485,8 @@
 
     @pl.when(signals)
     def _():
-        to_site[0].wait_send()
+        for copy in to_site[:2]:
+            copy.wait_send()
         pl.semaphore_signal(
             order_sem, inc=1, device_id=at(1 - 2 * core, 0), device_id_type=MESH
         )
@@ -475,27 +497,35 @@
         for copy in to_site:
             copy.start()
 
+    @pl.when(relays)
+    def _():
+        for arriving, onward in zip(to_relay, relay):
+            arriving.wait_recv()
+            onward.start()
+
     def state(slot, send_place, flow_step):
-        return remote(leaving.at[slot], arrived.at[1], (send_place, 11), at(flow_step, 0))
+        return remote(leaving.at[slot], arrived.at[1], (send_place, 23), at(flow_step, 0))
 
     sends = [
-        (flow == 27, state(1, 9, 4)),
-        (flow == 27, state(1, 10, 3)),
-        (odd & ~among(11, 13, 17, 23, 25, 29, 31), state(1, 11, 2)),
-        (odd & ~among(23, 25, 29, 31), state(1, 12, 1)),
+        (flow == 27, state(1, 13, 4)),
+        (flow == 27, state(1, 14, 3)),
+        (odd & ~among(11, 15, 17, 23, 25, 29, 31), state(1, 15, 2)),
+        (odd & ~among(15, 23, 25, 29, 31), state(1, 16, 1)),
     ]
     express_sends = [
-        (among(13, 21), state(0, 13, 6)),
-        (flow == 21, state(0, 14, 5)),
-        (among(9, 21), state(0, 15, 4)),
-        (flow == 21, state(0, 16, 3)),
-        (flow == 13, state(0, 17, 2)),
+        (among(13, 21), state(0, 17, 6)),
+        (flow == 21, state(0, 18, 5)),
+        (express, state(0, 19, 4)),
+        (among(13, 21), state(0, 20, 3)),
     ]
     receives_state = sends[0][1].wait_recv
 
     def passed(box):
-        offset = remote(offsets.at[2 + box], offsets.at[2 + box], (17 + box, 7 + box), at(-1, 0))
-        return in_halves(got.at[box], got.at[box], 18 + 2 * box, box, -1) + [offset]
+        first = 17 + 5 * box
+        offset = offsets.at[2 + box]
+        return in_parts(got.at[box], got.at[box], first, received(box), -1) + [
+            remote(offset, offset, (first + PARTS, 19 + box), at(-1, 0))
+        ]
 
     @pl.when(~inner)
     def _():
@@ -506,6 +536,7 @@
     @pl.when(inner)
     def _():
         base = jnp.where(odd, CHIP, OWN)
+        own_used = jnp.where(flow == 13, MORE + 1, CHIP)
 
         def compose(turn, carry):
             box = jnp.where(
@@ -517,9 +548,14 @@
             held_later = (turn == 0) | before | ((flow == 13) & (turn == 1))
             later = jnp.where(held_later, held, layer)
             earlier = jnp.where(held_later, layer, held)
-            for copy in in_halves(sent, got.at[box], 3, box, -1):
+
+            @pl.when(express & (turn == more))
+            def _():
+                pack_turned(turned.at[1], matrices[own_used])
+
+            for copy in in_parts(sent, got.at[box], 3, received(box), -1):
                 copy.wait_recv()
-            remote(own_offset, offsets.at[layer], (7, 7 + box), at(-1, 0)).wait_recv()
+            remote(own_offset, offsets.at[layer], (11, 19 + box), at(-1, 0)).wait_recv()
 
             @pl.when(passes & (turn > 0))
             def _():
@@ -533,13 +569,8 @@
 
         lax.fori_loop(1 - core, 1 + more, compose, 0)
 
-        own_used = jnp.where(flow == 13, MORE + 1, CHIP)
-        used = jnp.where(more > 0, MORE + more, jnp.where(odd & (flow != 15), CHIP, OWN))
+        used = jnp.where(more > 0, MORE + more, base)
         pack_turned(turned.at[0], matrices[used])
-
-        @pl.when(express)
-        def _():
-            pack_turned(turned.at[1], matrices[own_used])
 
         turns = jnp.where(express, 3, 2)
 
@@ -590,8 +621,10 @@
     for copy in to_second:
         pl.when(inner & ~odd)(copy.wait_send)
     pl.when(~odd)(offset_to_second.wait_send)
-    pl.when(helper & ~signals)(to_site[0].wait_send)
-    pl.when(helper)(to_site[1].wait_send)
+    for n, copy in enumerate(to_site):
+        pl.when(helper & ~signals if n < 2 else helper)(copy.wait_send)
+    for copy in relay:
+        pl.when(relays)(copy.wait_send)
     pl.when(helper)(offset_to_site.wait_send)
     for sends, _, halo in halos:
         pl.when(sends)(halo.wait_send)
@@ -624,8 +657,8 @@
             pltpu.VMEM((2, vectors, WIDE), F32),
             pltpu.VMEM((2, vectors, WIDE), F32),
             pltpu.SemaphoreType.DMA((26,)),
-            pltpu.SemaphoreType.DMA((24,)),
-            pltpu.SemaphoreType.DMA((16,)),
+            pltpu.SemaphoreType.DMA((36,)),
+            pltpu.SemaphoreType.DMA((28,)),
             pltpu.SemaphoreType.REGULAR,
         ],
         compiler_params=pltpu.CompilerParams(

time: 41.4 us -> 36.5 us (0.88); the launches traced: 41.2 us -> 35.8 us
  Pallas kernels: 39.8 us -> 34.4 us
    pallas_call x1, Pallas kernels: 39.8 us -> 34.4 us  [body(): pl.pallas_call(functools.partial(kernel, flows, crosses), out_shape=jax.S...]
where the time goes in v4:
time: 36.5 us; the launch traced here: 35.8 us
  Pallas kernels  34.4 us (94%)
  local copies, waits for them, and re-layouts  1.38 us (4%)
    pallas_call x1, Pallas kernels, body(): pl.pallas_call(functools.partial(kernel, flows, crosses), out_shape=jax.S...  34.4 us
    unnamed x1, local copies, waits for them, and re-layouts  1.38 us

profile of v4, /device:TPU:126, one launch (start us, length us, event | category | flops | bytes accessed | tf_op | source)
XLA Modules:
  0.0 35.8 jit_solution(7405260448798898200)
XLA Ops:
  0.0 34.4 %sweep_chain.1 = f32[1,2,2,8,135]{4,3,2,1,0:T(8,128)} custom-call(s32[1,2,2]{2,1,0:T(2,128)} %color_ref.1, f32[1,2,2,8,135]{4,3,2,1,0:T(8,128)} %rhs_hbm.1, f32[1,2,2,8,135]{4,3,2,1,0:T(8,128)} %old_hbm.1, f32[1,2,135,2,135]{4,3,2,1,0:T(2,128)} %bitcast.3, f32[1,6,2,135,2,135]{5,4,3,2,1,0:T(2,128)} %bitcast.2), custom_call_target="tpu_custom_call" | custom-call | flops 1000000000 | bytes 4000000 | tf_op jit(solution)/shard_map/sweep_chain/pallas_call | solution.py:636
  34.4 1.4 %copy.7 = f32[1,2,2,8,135]{4,3,2,1,0:T(8,128)} copy(f32[1,2,2,8,135]{4,3,2,1,0:T(8,128)} %sweep_chain.1) | data formatting | bytes 34560

commit v5 on v4

--- a/solution.py
+++ b/solution.py
@@ -20,7 +20,7 @@
 EDGE, SIDE, FLAG, SENT = 1024, 1088, 1224, 1248
 PARTS = 4
 PART = SENT // PARTS
-OWN, FIRST, CHIP, FAR, MORE = 0, 1, 2, 3, 5
+OWN, FIRST, CHIP, FAR, MORE = 0, 1, 2, 3, 6
 PLACES = (
     ((0, 2), (None, 4), (None, 5), None),
     ((4, None), (2, 0), None, (5, None)),
@@ -49,14 +49,11 @@
     return jnp.concatenate([high, rows - high], axis=0).astype(BF16)
 
 
-def times_halves(rows, high, low):
+def times_block(rows, block):
     both = stacked(rows)
+    high, low = halves(block)
     out = dot(both, high, NT) + dot(both, low, NT)
     return out[:8] + out[8:]
-
-
-def times_block(rows, block):
-    return times_halves(rows, *halves(block))
 
 
 def step(rows, weights):
@@ -165,12 +162,13 @@
 def kernel(
     flows,
     crosses,
-    color_ref,
+    color_hbm,
     rhs_hbm,
     old_hbm,
     inv_hbm,
     faces_hbm,
     out_ref,
+    colors,
     rhs,
     old,
     inv,
@@ -183,7 +181,6 @@
     matrices,
     offsets,
     parts,
-    blocks,
     weights,
     turned,
     arrived,
@@ -203,20 +200,28 @@
     def among(*layers):
         return functools.reduce(jnp.logical_or, [flow == layer for layer in layers])
 
-    before, express = among(19, 26, 27, 30, 31), among(9, 13, 21)
+    before, express = among(26, 27, 30, 31), among(9, 13, 19)
     more = jnp.where(
-        flow == 9, 1, jnp.where(flow == 13, 3, jnp.where(among(19, 21, 26, 27, 30, 31), 2, 0))
+        flow == 9,
+        1,
+        jnp.where(
+            flow == 13, 3, jnp.where(among(19, 27), 4, jnp.where(among(26, 30, 31), 2, 0))
+        ),
     )
     passes = among(27, 31)
-    helper = among(10, 11, 14, 15, 16, 17, 22, 23, 24, 25, 28, 29)
-    signals, goes_after = among(22, 25, 29), among(23, 24, 28)
+    helper = among(10, 11, 14, 15, 16, 17, 20, 21, 22, 23, 24, 25, 28, 29)
+    signals, goes_after = among(20, 23, 25, 29), among(21, 22, 24, 28)
     to_site_step = jnp.where(
-        among(10, 14, 22),
+        among(10, 14, 20),
         -1,
-        jnp.where(among(15, 23), -2, jnp.where(odd, 2, 3)),
-    )
+        jnp.where(
+            among(15, 21),
+            -2,
+            jnp.where(flow == 22, 5, jnp.where(flow == 23, 4, jnp.where(odd, 2, 3))),
+        ),
+    )
+    to_site_box = jnp.where(among(15, 20, 23), 3, jnp.where(among(21, 22), 4, 1 + core))
     relayed, relays = among(15, 16), among(4, 10)
-    to_site_box = jnp.where(flow == 15, 3, 1 + core)
 
     def at(flow_step, cross_step):
         return (flow + flow_step, cross + cross_step)
@@ -231,22 +236,16 @@
         (odd & (flow < flows - 2), at(2, 0)),
     ]
     for distance, layers in (
-        (3, (13, 16, 21, 24, 27, 28)),
-        (4, (9, 13, 21, 27)),
-        (5, (21,)),
-        (6, (10, 13, 21)),
+        (3, (13, 16, 19, 23, 24, 27, 28)),
+        (4, (9, 13, 19, 23, 27)),
+        (5, (22,)),
+        (6, (10, 13)),
+        (8, (19,)),
         (9, (4, 10)),
         (11, (4,)),
     ):
         partners.append((among(*layers), at(distance, 0)))
         partners.append((among(*(layer + distance for layer in layers)), at(-distance, 0)))
-    expected = 0
-    for present, device in partners:
-        expected = expected + present.astype(jnp.int32)
-
-        @pl.when(present)
-        def _(device=device):
-            pl.semaphore_signal(barrier, inc=1, device_id=device, device_id_type=MESH)
 
     def block_load(place, face, j, k):
         source = inv_hbm.at[0] if face is None else faces_hbm.at[0, face]
@@ -269,6 +268,8 @@
         count += len(group)
     old_load = pltpu.make_async_copy(old_hbm.at[0], old, load_sem.at[count])
     rhs_load = pltpu.make_async_copy(rhs_hbm.at[0], rhs, load_sem.at[count + 1])
+    color_load = pltpu.make_async_copy(color_hbm.at[0], colors, load_sem.at[count + 2])
+    color_load.start()
     old_load.start()
     rhs_load.start()
 
@@ -284,11 +285,16 @@
             for load in loads[n]:
                 load.start()
 
-    sent[...] = jnp.zeros_like(sent)
+    expected = 0
+    for present, device in partners:
+        expected = expected + present.astype(jnp.int32)
+
+        @pl.when(present)
+        def _(device=device):
+            pl.semaphore_signal(barrier, inc=1, device_id=device, device_id_type=MESH)
+
     offsets[OWN] = jnp.zeros((8, WIDE), F32)
     arrived[0] = jnp.zeros((8, WIDE), F32)
-    for slot in (OWN, FIRST, FAR, FAR + 1, FAR + 2):
-        matrices[slot, ROWS:] = jnp.zeros((WIDE - ROWS, WIDE), F32)
     pl.semaphore_wait(barrier, expected)
 
     def remote(source, target, places, device):
@@ -310,7 +316,8 @@
     for sends, _, halo in halos:
         pl.when(sends)(halo.start)
 
-    even = color_ref[0, 0, 0] == 0
+    color_load.wait()
+    even = colors[0, 0] == 0
 
     def pick(first, second):
         return jnp.where(even, first, second)
@@ -346,21 +353,23 @@
         sent,
         got.at[jnp.where(relayed, 1, to_site_box)],
         7,
-        jnp.where(relayed, 24, received(to_site_box)),
+        jnp.where(relayed, 29, received(to_site_box)),
         jnp.where(flow == 15, -11, jnp.where(flow == 16, -6, to_site_step)),
     )
     relay_box = jnp.where(flow == 4, 3, 1)
-    to_relay = in_parts(sent, got.at[1], 32, 24, -1)
+    to_relay = in_parts(sent, got.at[1], 32, 29, -1)
     relay = in_parts(got.at[1], got.at[relay_box], 32, received(relay_box), 9)
 
     @pl.when(~inner)
     def _():
-        for n in (0, 2):
-            for load in loads[n]:
-                load.wait()
+        for load in loads[2]:
+            load.wait()
 
     @pl.when(inner)
     def _():
+        sent[...] = jnp.zeros_like(sent)
+        for slot in (OWN, FIRST, FAR, FAR + 1, FAR + 2, FAR + 3):
+            matrices[slot, ROWS:] = jnp.zeros((WIDE - ROWS, WIDE), F32)
         for n in (0, 1):
             for load in loads[n]:
                 load.wait()
@@ -412,26 +421,6 @@
     for load in loads[3]:
         load.wait()
 
-    for e in range(4):
-        blocks[2 * e, 0], blocks[2 * e, 1] = halves(faces[1, e // 2, e % 2])
-        blocks[2 * e + 1, 0], blocks[2 * e + 1, 1] = halves(out_face(e))
-    for n, block in enumerate(
-        (
-            pick(inverse(0), inverse(1)),
-            pick(inverse(3), inverse(2)),
-            pick(cross_face(1), cross_face(0)),
-            pick(span_face(1), span_face(0)),
-            pick(cross_face(2), cross_face(3)),
-            pick(span_face(2), span_face(3)),
-            pick(inverse(1), inverse(0)),
-            pick(inverse(2), inverse(3)),
-        )
-    ):
-        blocks[8 + n, 0], blocks[8 + n, 1] = halves(block)
-
-    def times(rows, n):
-        return times_halves(rows, blocks[n, 0], blocks[n, 1])
-
     for _, receives, halo in halos:
         pl.when(receives)(halo.wait_recv)
 
@@ -441,17 +430,17 @@
         under = jnp.where(has_lower, below[j, k], 0.0)
         return (
             rhs[j, k]
-            - times(under, 2 * e)
-            - times(halo, 2 * e + 1)
+            - times_block(under, faces[1, j, k])
+            - times_block(halo, out_face(e))
         )
 
     for e in range(4):
         parts[e] = part(e)
 
     own_offset, first_offset = offsets.at[OWN], offsets.at[FIRST]
-    offset_to_second = remote(own_offset, first_offset, (11, 19), at(1, 0))
+    offset_to_second = remote(own_offset, first_offset, (11, 23), at(1, 0))
     offset_to_site = remote(
-        own_offset, offsets.at[2 + to_site_box], (12, 19 + to_site_box), at(to_site_step, 0)
+        own_offset, offsets.at[2 + to_site_box], (12, 23 + to_site_box), at(to_site_step, 0)
     )
 
     @pl.when(flow == 1)
@@ -471,10 +460,24 @@
 
     total_a = pick(parts[0], parts[1]) - around_a
     total_d = pick(parts[3], parts[2]) - around_d
-    new_a, new_d = times(total_a, 8), times(total_d, 9)
-    total_b = pick(parts[1], parts[0]) - (times(new_d, 10) + times(new_a, 11))
-    total_c = pick(parts[2], parts[3]) - (times(new_a, 12) + times(new_d, 13))
-    new_b, new_c = times(total_b, 14), times(total_c, 15)
+
+    @pl.when(~inner)
+    def _():
+        for load in loads[0]:
+            load.wait()
+
+    new_a = times_block(total_a, pick(inverse(0), inverse(1)))
+    new_d = times_block(total_d, pick(inverse(3), inverse(2)))
+    total_b = pick(parts[1], parts[0]) - (
+        times_block(new_d, pick(cross_face(1), cross_face(0)))
+        + times_block(new_a, pick(span_face(1), span_face(0)))
+    )
+    total_c = pick(parts[2], parts[3]) - (
+        times_block(new_a, pick(cross_face(2), cross_face(3)))
+        + times_block(new_d, pick(span_face(2), span_face(3)))
+    )
+    new_b = times_block(total_b, pick(inverse(1), inverse(0)))
+    new_c = times_block(total_c, pick(inverse(2), inverse(3)))
     put_rows(own_offset, 0, pick(new_a, new_b))
     put_rows(own_offset, 1, pick(new_b, new_a))
     put_rows(own_offset, 2, pick(new_c, new_d))
@@ -504,19 +507,19 @@
             onward.start()
 
     def state(slot, send_place, flow_step):
-        return remote(leaving.at[slot], arrived.at[1], (send_place, 23), at(flow_step, 0))
+        return remote(leaving.at[slot], arrived.at[1], (send_place, 28), at(flow_step, 0))
 
     sends = [
         (flow == 27, state(1, 13, 4)),
-        (flow == 27, state(1, 14, 3)),
-        (odd & ~among(11, 15, 17, 23, 25, 29, 31), state(1, 15, 2)),
-        (odd & ~among(15, 23, 25, 29, 31), state(1, 16, 1)),
+        (among(23, 27), state(1, 14, 3)),
+        (odd & ~among(11, 15, 17, 21, 25, 29, 31), state(1, 15, 2)),
+        (odd & ~among(15, 21, 25, 29, 31), state(1, 16, 1)),
     ]
     express_sends = [
-        (among(13, 21), state(0, 17, 6)),
-        (flow == 21, state(0, 18, 5)),
+        (flow == 19, state(0, 17, 8)),
+        (flow == 13, state(0, 18, 6)),
         (express, state(0, 19, 4)),
-        (among(13, 21), state(0, 20, 3)),
+        (among(13, 19), state(0, 20, 3)),
     ]
     receives_state = sends[0][1].wait_recv
 
@@ -524,7 +527,7 @@
         first = 17 + 5 * box
         offset = offsets.at[2 + box]
         return in_parts(got.at[box], got.at[box], first, received(box), -1) + [
-            remote(offset, offset, (first + PARTS, 19 + box), at(-1, 0))
+            remote(offset, offset, (first + PARTS, 23 + box), at(-1, 0))
         ]
 
     @pl.when(~inner)
@@ -536,16 +539,16 @@
     @pl.when(inner)
     def _():
         base = jnp.where(odd, CHIP, OWN)
-        own_used = jnp.where(flow == 13, MORE + 1, CHIP)
+        own_used = jnp.where(flow == 13, MORE + 1, jnp.where(flow == 19, MORE + 2, CHIP))
 
         def compose(turn, carry):
-            box = jnp.where(
-                (turn == 0) | (turn == 3) | among(9, 21), turn, 3 - turn
-            )
+            box = jnp.where((turn == 0) | (turn >= 3) | (flow == 9), turn, 3 - turn)
             layer = jnp.where(turn == 0, FIRST, 2 + box)
             held = jnp.where(turn == 0, OWN, jnp.where(turn == 1, base, MORE - 1 + turn))
             result = jnp.where(turn == 0, CHIP, MORE + turn)
-            held_later = (turn == 0) | before | ((flow == 13) & (turn == 1))
+            held_later = (
+                (turn == 0) | before | ((flow == 13) & (turn == 1)) | ((flow == 19) & (turn <= 2))
+            )
             later = jnp.where(held_later, held, layer)
             earlier = jnp.where(held_later, layer, held)
 
@@ -555,9 +558,9 @@
 
             for copy in in_parts(sent, got.at[box], 3, received(box), -1):
                 copy.wait_recv()
-            remote(own_offset, offsets.at[layer], (11, 19 + box), at(-1, 0)).wait_recv()
-
-            @pl.when(passes & (turn > 0))
+            remote(own_offset, offsets.at[layer], (11, 23 + box), at(-1, 0)).wait_recv()
+
+            @pl.when(passes & (turn > 0) & (turn < 3))
             def _():
                 for copy in passed(box):
                     copy.start()
@@ -636,9 +639,10 @@
     return pl.pallas_call(
         functools.partial(kernel, flows, crosses),
         out_shape=jax.ShapeDtypeStruct(right_side.shape, F32),
-        in_specs=[pl.BlockSpec(memory_space=pltpu.SMEM), hbm, hbm, hbm, hbm],
+        in_specs=[hbm] * 5,
         out_specs=pl.BlockSpec(memory_space=pltpu.VMEM),
         scratch_shapes=[
+            pltpu.SMEM((columns, spans), jnp.int32),
             pltpu.VMEM((columns, spans, vectors, width), F32),
             pltpu.VMEM((columns, spans, vectors, width), F32),
             pltpu.VMEM((columns, spans, width, width), F32),
@@ -647,22 +651,21 @@
             pltpu.VMEM((spans, vectors, width), F32),
             pltpu.VMEM((columns, spans, vectors, width), F32),
             pltpu.VMEM((SENT, 128), F32),
-            pltpu.VMEM((4, SENT, 128), F32),
-            pltpu.VMEM((9, WIDE, WIDE), F32),
-            pltpu.VMEM((9, vectors, WIDE), F32),
+            pltpu.VMEM((5, SENT, 128), F32),
+            pltpu.VMEM((11, WIDE, WIDE), F32),
+            pltpu.VMEM((11, vectors, WIDE), F32),
             pltpu.VMEM((2 * columns, vectors, width), F32),
-            pltpu.VMEM((16, 2, width, width), BF16),
             pltpu.VMEM((WIDE, DEEP), BF16),
             pltpu.VMEM((2, DEEP, WIDE), BF16),
             pltpu.VMEM((2, vectors, WIDE), F32),
             pltpu.VMEM((2, vectors, WIDE), F32),
-            pltpu.SemaphoreType.DMA((26,)),
+            pltpu.SemaphoreType.DMA((27,)),
             pltpu.SemaphoreType.DMA((36,)),
-            pltpu.SemaphoreType.DMA((28,)),
+            pltpu.SemaphoreType.DMA((33,)),
             pltpu.SemaphoreType.REGULAR,
         ],
         compiler_params=pltpu.CompilerParams(
-            collective_id=0, has_side_effects=True, vmem_limit_bytes=60 * 1024 * 1024
+            collective_id=0, has_side_effects=True, vmem_limit_bytes=(54 * 1024 - 128) * 1024
         ),
         cost_estimate=pl.CostEstimate(flops=10**9, bytes_accessed=4 * 10**6, transcendentals=0),
         name="sweep_chain",

time: 36.5 us -> 37.2 us (1.019)
  the two profiles are of different devices: /device:TPU:126 before, /device:TPU:102 now
where the time goes in v5:
time: 37.2 us; the launch traced here: 37.1 us
  Pallas kernels  35.8 us (96%)
  local copies, waits for them, and re-layouts  1.3 us (3%)
    pallas_call x1, Pallas kernels, body(): pl.pallas_call(functools.partial(kernel, flows, crosses), out_shape=jax.S...  35.8 us
    unnamed x3, local copies, waits for them, and re-layouts  1.3 us

profile of v5, /device:TPU:102, one launch (start us, length us, event | category | flops | bytes accessed | tf_op | source)
XLA Modules:
  0.0 37.1 jit_solution(9670441717481999237)
XLA Ops:
  0.0 0.0 copy-start
  0.0 0.7 %copy-done = s32[1,2,2]{2,1,0:T(2,128)S(1)} copy-done((s32[1,2,2]{2,1,0:T(2,128)S(1)}, s32[1,2,2]{2,1,0:T(2,128)}, u32[]{:S(2)}) %copy-start) | copy-done | bytes 40
  0.7 35.8 %sweep_chain.1 = f32[1,2,2,8,135]{4,3,2,1,0:T(8,128)S(1)} custom-call(s32[1,2,2]{2,1,0:T(2,128)S(1)} %copy-done, f32[1,2,2,8,135]{4,3,2,1,0:T(8,128)} %rhs_hbm.1, f32[1,2,2,8,135]{4,3,2,1,0:T(8,128)} %old_hbm.1, f32[1,2,135,2,135]{4,3,2,1,0:T(2,128)} %bitcast.3, f32[1,6,2,135,2,135]{5,4,3,2,1,0:T(2,128)} %bitcast.2), custom_call_target="tpu_custom_call" | custom-call | flops 1000000000 | bytes 4000000 | tf_op jit(solution)/shard_map/sweep_chain/pallas_call | solution.py:639
  36.5 0.6 %copy.7 = f32[1,2,2,8,135]{4,3,2,1,0:T(8,128)} copy(f32[1,2,2,8,135]{4,3,2,1,0:T(8,128)S(1)} %sweep_chain.1) | data formatting | bytes 34560
Async XLA Ops:
  0.0 0.7 %copy-start = (s32[1,2,2]{2,1,0:T(2,128)S(1)}, s32[1,2,2]{2,1,0:T(2,128)}, u32[]{:S(2)}) copy-start(s32[1,2,2]{2,1,0:T(2,128)} %color_hbm.1) | copy-start | bytes 52

commit v6 on v5

--- a/solution.py
+++ b/solution.py
@@ -20,7 +20,7 @@
 EDGE, SIDE, FLAG, SENT = 1024, 1088, 1224, 1248
 PARTS = 4
 PART = SENT // PARTS
-OWN, FIRST, CHIP, FAR, MORE = 0, 1, 2, 3, 6
+OWN, FIRST, CHIP, FAR, MORE = 0, 1, 2, 3, 5
 PLACES = (
     ((0, 2), (None, 4), (None, 5), None),
     ((4, None), (2, 0), None, (5, None)),
@@ -200,28 +200,20 @@
     def among(*layers):
         return functools.reduce(jnp.logical_or, [flow == layer for layer in layers])
 
-    before, express = among(26, 27, 30, 31), among(9, 13, 19)
+    before, express = among(19, 26, 27, 30, 31), among(9, 13, 21)
     more = jnp.where(
-        flow == 9,
-        1,
-        jnp.where(
-            flow == 13, 3, jnp.where(among(19, 27), 4, jnp.where(among(26, 30, 31), 2, 0))
-        ),
+        flow == 9, 1, jnp.where(flow == 13, 3, jnp.where(among(19, 21, 26, 27, 30, 31), 2, 0))
     )
     passes = among(27, 31)
-    helper = among(10, 11, 14, 15, 16, 17, 20, 21, 22, 23, 24, 25, 28, 29)
-    signals, goes_after = among(20, 23, 25, 29), among(21, 22, 24, 28)
+    helper = among(10, 11, 14, 15, 16, 17, 22, 23, 24, 25, 28, 29)
+    signals, goes_after = among(22, 25, 29), among(23, 24, 28)
     to_site_step = jnp.where(
-        among(10, 14, 20),
+        among(10, 14, 22),
         -1,
-        jnp.where(
-            among(15, 21),
-            -2,
-            jnp.where(flow == 22, 5, jnp.where(flow == 23, 4, jnp.where(odd, 2, 3))),
-        ),
-    )
-    to_site_box = jnp.where(among(15, 20, 23), 3, jnp.where(among(21, 22), 4, 1 + core))
+        jnp.where(among(15, 23), -2, jnp.where(odd, 2, 3)),
+    )
     relayed, relays = among(15, 16), among(4, 10)
+    to_site_box = jnp.where(flow == 15, 3, 1 + core)
 
     def at(flow_step, cross_step):
         return (flow + flow_step, cross + cross_step)
@@ -236,11 +228,10 @@
         (odd & (flow < flows - 2), at(2, 0)),
     ]
     for distance, layers in (
-        (3, (13, 16, 19, 23, 24, 27, 28)),
-        (4, (9, 13, 19, 23, 27)),
-        (5, (22,)),
-        (6, (10, 13)),
-        (8, (19,)),
+        (3, (13, 16, 21, 24, 27, 28)),
+        (4, (9, 13, 21, 27)),
+        (5, (21,)),
+        (6, (10, 13, 21)),
         (9, (4, 10)),
         (11, (4,)),
     ):
@@ -368,7 +359,7 @@
     @pl.when(inner)
     def _():
         sent[...] = jnp.zeros_like(sent)
-        for slot in (OWN, FIRST, FAR, FAR + 1, FAR + 2, FAR + 3):
+        for slot in (OWN, FIRST, FAR, FAR + 1, FAR + 2):
             matrices[slot, ROWS:] = jnp.zeros((WIDE - ROWS, WIDE), F32)
         for n in (0, 1):
             for load in loads[n]:
@@ -511,15 +502,15 @@
 
     sends = [
         (flow == 27, state(1, 13, 4)),
-        (among(23, 27), state(1, 14, 3)),
-        (odd & ~among(11, 15, 17, 21, 25, 29, 31), state(1, 15, 2)),
-        (odd & ~among(15, 21, 25, 29, 31), state(1, 16, 1)),
+        (flow == 27, state(1, 14, 3)),
+        (odd & ~among(11, 15, 17, 23, 25, 29, 31), state(1, 15, 2)),
+        (odd & ~among(15, 23, 25, 29, 31), state(1, 16, 1)),
     ]
     express_sends = [
-        (flow == 19, state(0, 17, 8)),
-        (flow == 13, state(0, 18, 6)),
+        (among(13, 21), state(0, 17, 6)),
+        (flow == 21, state(0, 18, 5)),
         (express, state(0, 19, 4)),
-        (among(13, 19), state(0, 20, 3)),
+        (among(13, 21), state(0, 20, 3)),
     ]
     receives_state = sends[0][1].wait_recv
 
@@ -539,16 +530,14 @@
     @pl.when(inner)
     def _():
         base = jnp.where(odd, CHIP, OWN)
-        own_used = jnp.where(flow == 13, MORE + 1, jnp.where(flow == 19, MORE + 2, CHIP))
+        own_used = jnp.where(flow == 13, MORE + 1, CHIP)
 
         def compose(turn, carry):
-            box = jnp.where((turn == 0) | (turn >= 3) | (flow == 9), turn, 3 - turn)
+            box = jnp.where((turn == 0) | (turn == 3) | among(9, 21), turn, 3 - turn)
             layer = jnp.where(turn == 0, FIRST, 2 + box)
             held = jnp.where(turn == 0, OWN, jnp.where(turn == 1, base, MORE - 1 + turn))
             result = jnp.where(turn == 0, CHIP, MORE + turn)
-            held_later = (
-                (turn == 0) | before | ((flow == 13) & (turn == 1)) | ((flow == 19) & (turn <= 2))
-            )
+            held_later = (turn == 0) | before | ((flow == 13) & (turn == 1))
             later = jnp.where(held_later, held, layer)
             earlier = jnp.where(held_later, layer, held)
 
@@ -560,7 +549,7 @@
                 copy.wait_recv()
             remote(own_offset, offsets.at[layer], (11, 23 + box), at(-1, 0)).wait_recv()
 
-            @pl.when(passes & (turn > 0) & (turn < 3))
+            @pl.when(passes & (turn > 0))
             def _():
                 for copy in passed(box):
                     copy.start()
@@ -651,9 +640,9 @@
             pltpu.VMEM((spans, vectors, width), F32),
             pltpu.VMEM((columns, spans, vectors, width), F32),
             pltpu.VMEM((SENT, 128), F32),
-            pltpu.VMEM((5, SENT, 128), F32),
-            pltpu.VMEM((11, WIDE, WIDE), F32),
-            pltpu.VMEM((11, vectors, WIDE), F32),
+            pltpu.VMEM((4, SENT, 128), F32),
+            pltpu.VMEM((9, WIDE, WIDE), F32),
+            pltpu.VMEM((9, vectors, WIDE), F32),
             pltpu.VMEM((2 * columns, vectors, width), F32),
             pltpu.VMEM((WIDE, DEEP), BF16),
             pltpu.VMEM((2, DEEP, WIDE), BF16),

time: 37.2 us -> 35.2 us (0.946)
  the two profiles are of different devices: /device:TPU:102 before, /device:TPU:126 now
where the time goes in v6:
time: 35.2 us; the launch traced here: 34.7 us
  Pallas kernels  33.4 us (95%)
  local copies, waits for them, and re-layouts  1.3 us (4%)
    pallas_call x1, Pallas kernels, body(): pl.pallas_call(functools.partial(kernel, flows, crosses), out_shape=jax.S...  33.4 us
    unnamed x3, local copies, waits for them, and re-layouts  1.3 us

profile of v6, /device:TPU:126, one launch (start us, length us, event | category | flops | bytes accessed | tf_op | source)
XLA Modules:
  0.0 34.7 jit_solution(4567214142073234889)
XLA Ops:
  0.0 0.0 copy-start
  0.0 0.7 %copy-done = s32[1,2,2]{2,1,0:T(2,128)S(1)} copy-done((s32[1,2,2]{2,1,0:T(2,128)S(1)}, s32[1,2,2]{2,1,0:T(2,128)}, u32[]{:S(2)}) %copy-start) | copy-done | bytes 40
  0.7 33.4 %sweep_chain.1 = f32[1,2,2,8,135]{4,3,2,1,0:T(8,128)S(1)} custom-call(s32[1,2,2]{2,1,0:T(2,128)S(1)} %copy-done, f32[1,2,2,8,135]{4,3,2,1,0:T(8,128)} %rhs_hbm.1, f32[1,2,2,8,135]{4,3,2,1,0:T(8,128)} %old_hbm.1, f32[1,2,135,2,135]{4,3,2,1,0:T(2,128)} %bitcast.3, f32[1,6,2,135,2,135]{5,4,3,2,1,0:T(2,128)} %bitcast.2), custom_call_target="tpu_custom_call" | custom-call | flops 1000000000 | bytes 4000000 | tf_op jit(solution)/shard_map/sweep_chain/pallas_call | solution.py:628
  34.0 0.6 %copy.7 = f32[1,2,2,8,135]{4,3,2,1,0:T(8,128)} copy(f32[1,2,2,8,135]{4,3,2,1,0:T(8,128)S(1)} %sweep_chain.1) | data formatting | bytes 34560
Async XLA Ops:
  0.0 0.7 %copy-start = (s32[1,2,2]{2,1,0:T(2,128)S(1)}, s32[1,2,2]{2,1,0:T(2,128)}, u32[]{:S(2)}) copy-start(s32[1,2,2]{2,1,0:T(2,128)} %color_hbm.1) | copy-start | bytes 52

commit v7 on v6

--- a/solution.py
+++ b/solution.py
@@ -189,6 +189,8 @@
     send_sem,
     recv_sem,
     order_sem,
+    ready_right,
+    ready_later,
 ):
     flow, cross = lax.axis_index("flow"), lax.axis_index("cross")
     core = lax.rem(flow, 2)
@@ -219,14 +221,8 @@
         return (flow + flow_step, cross + cross_step)
 
     barrier = pltpu.get_barrier_semaphore()
-    partners = [
-        (has_upper, at(-1, 0)),
-        (has_lower, at(1, 0)),
-        (has_left, at(0, -1)),
-        (has_right, at(0, 1)),
-        (odd & (flow >= 2), at(-2, 0)),
-        (odd & (flow < flows - 2), at(2, 0)),
-    ]
+    earlier_ones = [(has_upper, at(-1, 0)), (odd & (flow >= 2), at(-2, 0))]
+    later_ones = [(has_lower, at(1, 0)), (odd & (flow < flows - 2), at(2, 0))]
     for distance, layers in (
         (3, (13, 16, 21, 24, 27, 28)),
         (4, (9, 13, 21, 27)),
@@ -235,8 +231,8 @@
         (9, (4, 10)),
         (11, (4,)),
     ):
-        partners.append((among(*layers), at(distance, 0)))
-        partners.append((among(*(layer + distance for layer in layers)), at(-distance, 0)))
+        later_ones.append((among(*layers), at(distance, 0)))
+        earlier_ones.append((among(*(layer + distance for layer in layers)), at(-distance, 0)))
 
     def block_load(place, face, j, k):
         source = inv_hbm.at[0] if face is None else faces_hbm.at[0, face]
@@ -276,17 +272,26 @@
             for load in loads[n]:
                 load.start()
 
-    expected = 0
-    for present, device in partners:
-        expected = expected + present.astype(jnp.int32)
-
-        @pl.when(present)
-        def _(device=device):
-            pl.semaphore_signal(barrier, inc=1, device_id=device, device_id_type=MESH)
+    def counted(devices):
+        return sum(present.astype(jnp.int32) for present, _ in devices)
+
+    def tell(semaphore, devices):
+        for present, device in devices:
+
+            @pl.when(present)
+            def _(device=device):
+                pl.semaphore_signal(
+                    semaphore, inc=1, device_id=device, device_id_type=MESH
+                )
+
+    tell(barrier, [(has_right, at(0, 1))] + later_ones)
 
     offsets[OWN] = jnp.zeros((8, WIDE), F32)
-    arrived[0] = jnp.zeros((8, WIDE), F32)
-    pl.semaphore_wait(barrier, expected)
+    @pl.when(has_left | has_upper)
+    def _():
+        pl.semaphore_wait(barrier, has_left.astype(jnp.int32) + counted(earlier_ones))
+
+    tell(ready_right, [(has_left, at(0, -1))])
 
     def remote(source, target, places, device):
         sending, receiving = places if isinstance(places, tuple) else (places, places)
@@ -304,8 +309,14 @@
         (has_left, has_right, remote(old_hbm.at[0, 0], halo_right, 1, at(0, -1))),
         (has_upper, has_lower, remote(old_hbm.at[0], below, 2, at(-1, 0))),
     ]
-    for sends, _, halo in halos:
+    for sends, _, halo in halos[1:]:
         pl.when(sends)(halo.start)
+    tell(ready_later, earlier_ones)
+
+    @pl.when(has_right)
+    def _():
+        pl.semaphore_wait(ready_right, 1)
+        halos[0][2].start()
 
     color_load.wait()
     even = colors[0, 0] == 0
@@ -391,6 +402,10 @@
             put_side(sent, *here, pick(block, nothing))
             put_side(sent, *there, pick(nothing, block))
         sent[FLAG:] = jnp.where(even, 1.0, 0.0) + jnp.zeros((SENT - FLAG, 128), F32)
+        @pl.when(has_lower)
+        def _():
+            pl.semaphore_wait(ready_later, counted(later_ones))
+
         for copy in to_site:
             pl.when(helper & ~goes_after)(copy.start)
         for copy in to_second:
@@ -474,6 +489,10 @@
     put_rows(own_offset, 2, pick(new_c, new_d))
     put_rows(own_offset, 3, pick(new_d, new_c))
 
+    @pl.when(~inner)
+    def _():
+        pl.semaphore_wait(ready_later, counted(later_ones))
+
     pl.when(~odd)(offset_to_second.start)
     pl.when(helper)(offset_to_site.start)
 
@@ -498,7 +517,7 @@
             onward.start()
 
     def state(slot, send_place, flow_step):
-        return remote(leaving.at[slot], arrived.at[1], (send_place, 28), at(flow_step, 0))
+        return remote(leaving.at[slot], arrived, (send_place, 28), at(flow_step, 0))
 
     sends = [
         (flow == 27, state(1, 13, 4)),
@@ -570,7 +589,7 @@
             pl.when(turn == 1)(receives_state)
             last = turn == turns - 1
             own = express & last
-            rows = arrived[jnp.where(turn == 0, 0, 1)]
+            rows = arrived[...]
             moved = fast_step(rows, turned.at[jnp.where(own, 1, 0)])
             leaving[jnp.where(last, 1, 0)] = moved + offsets[jnp.where(own, own_used, used)]
 
@@ -586,7 +605,7 @@
 
             return carry
 
-        lax.fori_loop(0, turns, advance, 0)
+        lax.fori_loop(1, turns, advance, 0)
 
     rows = leaving[1]
     for e in range(4):
@@ -646,11 +665,13 @@
             pltpu.VMEM((2 * columns, vectors, width), F32),
             pltpu.VMEM((WIDE, DEEP), BF16),
             pltpu.VMEM((2, DEEP, WIDE), BF16),
-            pltpu.VMEM((2, vectors, WIDE), F32),
+            pltpu.VMEM((vectors, WIDE), F32),
             pltpu.VMEM((2, vectors, WIDE), F32),
             pltpu.SemaphoreType.DMA((27,)),
             pltpu.SemaphoreType.DMA((36,)),
             pltpu.SemaphoreType.DMA((33,)),
+            pltpu.SemaphoreType.REGULAR,
+            pltpu.SemaphoreType.REGULAR,
             pltpu.SemaphoreType.REGULAR,
         ],
         compiler_params=pltpu.CompilerParams(

time: 35.2 us -> 34.9 us (level); the launches traced: 34.7 us -> 34.8 us
  no operation moved by 1% of the time
where the time goes in v7:
time: 34.9 us; the launch traced here: 34.8 us
  Pallas kernels  33.4 us (96%)
  local copies, waits for them, and re-layouts  1.3 us (4%)
    pallas_call x1, Pallas kernels, body(): pl.pallas_call(functools.partial(kernel, flows, crosses), out_shape=jax.S...  33.4 us
    unnamed x3, local copies, waits for them, and re-layouts  1.3 us

profile of v7, /device:TPU:126, one launch (start us, length us, event | category | flops | bytes accessed | tf_op | source)
XLA Modules:
  0.0 34.8 jit_solution(2411274105605025098)
XLA Ops:
  0.0 0.0 copy-start
  0.0 0.7 %copy-done = s32[1,2,2]{2,1,0:T(2,128)S(1)} copy-done((s32[1,2,2]{2,1,0:T(2,128)S(1)}, s32[1,2,2]{2,1,0:T(2,128)}, u32[]{:S(2)}) %copy-start) | copy-done | bytes 40
  0.7 33.4 %sweep_chain.1 = f32[1,2,2,8,135]{4,3,2,1,0:T(8,128)S(1)} custom-call(s32[1,2,2]{2,1,0:T(2,128)S(1)} %copy-done, f32[1,2,2,8,135]{4,3,2,1,0:T(8,128)} %rhs_hbm.1, f32[1,2,2,8,135]{4,3,2,1,0:T(8,128)} %old_hbm.1, f32[1,2,135,2,135]{4,3,2,1,0:T(2,128)} %bitcast.3, f32[1,6,2,135,2,135]{5,4,3,2,1,0:T(2,128)} %bitcast.2), custom_call_target="tpu_custom_call" | custom-call | flops 1000000000 | bytes 4000000 | tf_op jit(solution)/shard_map/sweep_chain/pallas_call | solution.py:647
  34.1 0.6 %copy.7 = f32[1,2,2,8,135]{4,3,2,1,0:T(8,128)} copy(f32[1,2,2,8,135]{4,3,2,1,0:T(8,128)S(1)} %sweep_chain.1) | data formatting | bytes 34560
Async XLA Ops:
  0.0 0.7 %copy-start = (s32[1,2,2]{2,1,0:T(2,128)S(1)}, s32[1,2,2]{2,1,0:T(2,128)}, u32[]{:S(2)}) copy-start(s32[1,2,2]{2,1,0:T(2,128)} %color_hbm.1) | copy-start | bytes 52

commit v8 on v7

--- a/solution.py
+++ b/solution.py
@@ -110,10 +110,10 @@
     tail_high, tail_low = high[MAIN:ROWS], low[MAIN:ROWS]
     tail = jnp.concatenate([tail_high, tail_high, tail_low, jnp.zeros_like(tail_high)], axis=0)
     return (
-        dot(weights[:, :MAIN], high[:MAIN], NN)
-        + dot(weights[:, :MAIN], low[:MAIN], NN)
-        + dot(weights[:, MAIN : 2 * MAIN], high[:MAIN], NN)
-        + dot(weights[:, 2 * MAIN :], tail, NN)
+        dot(weights[:TWICE, :MAIN], high[:MAIN], NN)
+        + dot(weights[:TWICE, :MAIN], low[:MAIN], NN)
+        + dot(weights[:TWICE, MAIN : 2 * MAIN], high[:MAIN], NN)
+        + dot(weights[:TWICE, 2 * MAIN :], tail, NN)
     )
 
 
@@ -372,6 +372,8 @@
         sent[...] = jnp.zeros_like(sent)
         for slot in (OWN, FIRST, FAR, FAR + 1, FAR + 2):
             matrices[slot, ROWS:] = jnp.zeros((WIDE - ROWS, WIDE), F32)
+        for slot in (CHIP, MORE + 1, MORE + 2, MORE + 3):
+            matrices[slot, TWICE:] = jnp.zeros((WIDE - TWICE, WIDE), F32)
         for n in (0, 1):
             for load in loads[n]:
                 load.wait()
@@ -559,11 +561,6 @@
             held_later = (turn == 0) | before | ((flow == 13) & (turn == 1))
             later = jnp.where(held_later, held, layer)
             earlier = jnp.where(held_later, layer, held)
-
-            @pl.when(express & (turn == more))
-            def _():
-                pack_turned(turned.at[1], matrices[own_used])
-
             for copy in in_parts(sent, got.at[box], 3, received(box), -1):
                 copy.wait_recv()
             remote(own_offset, offsets.at[layer], (11, 23 + box), at(-1, 0)).wait_recv()
@@ -574,7 +571,7 @@
                     copy.start()
 
             spread(matrices.at[layer], got.at[box])
-            matrices[result] = composed(weights, matrices[later], matrices[earlier])
+            matrices[result, :TWICE] = composed(weights, matrices[later], matrices[earlier])
             offsets[result] = step(offsets[earlier], weights[...]) + offsets[later]
             return carry
 
@@ -589,6 +586,11 @@
             pl.when(turn == 1)(receives_state)
             last = turn == turns - 1
             own = express & last
+
+            @pl.when(own)
+            def _():
+                pack_turned(turned.at[1], matrices[own_used])
+
             rows = arrived[...]
             moved = fast_step(rows, turned.at[jnp.where(own, 1, 0)])
             leaving[jnp.where(last, 1, 0)] = moved + offsets[jnp.where(own, own_used, used)]

time: 34.9 us -> 34.7 us (level)
  no operation moved by 1% of the time
where the time goes in v8:
time: 34.7 us; the launch traced here: 34.6 us
  Pallas kernels  33.3 us (96%)
  local copies, waits for them, and re-layouts  1.3 us (4%)
    pallas_call x1, Pallas kernels, body(): pl.pallas_call(functools.partial(kernel, flows, crosses), out_shape=jax.S...  33.3 us
    unnamed x3, local copies, waits for them, and re-layouts  1.3 us

profile of v8, /device:TPU:126, one launch (start us, length us, event | category | flops | bytes accessed | tf_op | source)
XLA Modules:
  0.0 34.6 jit_solution(15715323679786332019)
XLA Ops:
  0.0 0.0 copy-start
  0.0 0.7 %copy-done = s32[1,2,2]{2,1,0:T(2,128)S(1)} copy-done((s32[1,2,2]{2,1,0:T(2,128)S(1)}, s32[1,2,2]{2,1,0:T(2,128)}, u32[]{:S(2)}) %copy-start) | copy-done | bytes 40
  0.7 33.3 %sweep_chain.1 = f32[1,2,2,8,135]{4,3,2,1,0:T(8,128)S(1)} custom-call(s32[1,2,2]{2,1,0:T(2,128)S(1)} %copy-done, f32[1,2,2,8,135]{4,3,2,1,0:T(8,128)} %rhs_hbm.1, f32[1,2,2,8,135]{4,3,2,1,0:T(8,128)} %old_hbm.1, f32[1,2,135,2,135]{4,3,2,1,0:T(2,128)} %bitcast.3, f32[1,6,2,135,2,135]{5,4,3,2,1,0:T(2,128)} %bitcast.2), custom_call_target="tpu_custom_call" | custom-call | flops 1000000000 | bytes 4000000 | tf_op jit(solution)/shard_map/sweep_chain/pallas_call | solution.py:649
  34.0 0.6 %copy.7 = f32[1,2,2,8,135]{4,3,2,1,0:T(8,128)} copy(f32[1,2,2,8,135]{4,3,2,1,0:T(8,128)S(1)} %sweep_chain.1) | data formatting | bytes 34560
Async XLA Ops:
  0.0 0.7 %copy-start = (s32[1,2,2]{2,1,0:T(2,128)S(1)}, s32[1,2,2]{2,1,0:T(2,128)}, u32[]{:S(2)}) copy-start(s32[1,2,2]{2,1,0:T(2,128)} %color_hbm.1) | copy-start | bytes 52
